TPU v7x, 512 devices: a whole 4x4x16 slice. The times are simulated.
512 devices in a mesh: gx: 32 (over y, z_hi, core), gy: 16 (over x, z_lo).
Axes of the slice: x: 4, y: 4, z: 16 (z_hi: 4, z_lo: 4; z = z_hi * 4 + z_lo), core: 2. Of those that a mesh axis runs over, the one named last changes fastest.
Arguments:
- surface_tags: int32 [64, 128, 128], P('gx', 'gy'), may hold values from 0 to 16
- normal_index: int32 [64, 128, 128], P('gx', 'gy'), may hold values from 0 to 25
- fluid_mask: int32 [64, 128, 128], P('gx', 'gy'), may hold values 0 or 1
- body_centers: float32 [16, 3], replicated, may hold values from 0.25 to 0.75
Outputs:
- pressure: float32 [96, 64, 128, 128], P(None, 'gx', 'gy')
- added_mass: float32 [96, 96], replicated
Inputs may be any that keep to these rules, and one draw needn't show every extreme that they name: `surface_tags`: 16 marks a cell on no body's surface.
All inputs are finite; a program needn't handle non-finite values. No bound on the sum of `fluid_mask` on one device may be relied on, other than what follows from the above.
Results may differ from a plain program's by a relative error of at most 0.00005.
Values sent between devices are 32-bit elements; how exact they have to be, the bound alone decides.
No kernel may reach another device: no remote copies, remote signals or barrier semaphores. Data moves between devices by JAX's collectives and lax.ppermute only.
A program may use at most 64 MiB of HBM per device.

v0:
```python
import jax
import jax.numpy as jnp
from jax import lax
from jax.sharding import PartitionSpec as P

BODIES = 16


def extended(array, sides, width):
    for axis, dim in sides:
        size, length = (lax.axis_size(axis), array.shape[dim])
        up = [(i, (i + 1) % size) for i in range(size - 1)]
        down = [(j, i) for i, j in up]
        last = lax.slice_in_dim(array, length - width, length, axis=dim)
        first = lax.slice_in_dim(array, 0, width, axis=dim)
        before = lax.ppermute(last, axis, up)
        after = lax.ppermute(first, axis, down)
        array = jnp.concatenate([before, array, after], axis=dim)
    return array


def normals_of(index):
    shifted = index + (index >= 13).astype(jnp.int32)
    comp_x = (shifted // 9 - 1).astype(jnp.float32)
    comp_y = (shifted // 3 % 3 - 1).astype(jnp.float32)
    comp_z = (shifted % 3 - 1).astype(jnp.float32)
    length = jnp.sqrt(comp_x * comp_x + comp_y * comp_y + comp_z * comp_z)
    return (comp_x / length, comp_y / length, comp_z / length)


def forcing_of(tags, index, fluid, centers, pos_x, pos_y, pos_z):
    n_x, n_y, n_z = normals_of(index)
    shape = (BODIES,) + tags.shape
    bodies = jnp.arange(BODIES, dtype=jnp.int32)
    onehot = (tags[None] == bodies[:, None, None, None]).astype(jnp.float32) * fluid[None]
    lever_x = 3.0 * (pos_x[None, :, None, None] - centers[:, 0][:, None, None, None])
    lever_y = 3.0 * (pos_y[None, None, :, None] - centers[:, 1][:, None, None, None])
    lever_z = 3.0 * (pos_z[None, None, None, :] - centers[:, 2][:, None, None, None])
    parts = [
        n_x[None],
        n_y[None],
        n_z[None],
        lever_y * n_z[None] - lever_z * n_y[None],
        lever_z * n_x[None] - lever_x * n_z[None],
        lever_x * n_y[None] - lever_y * n_x[None],
    ]
    modes = jnp.stack([jnp.broadcast_to(part, shape) for part in parts], axis=1)
    modes = modes * onehot[:, None]
    return modes.reshape((6 * BODIES,) + tags.shape)


def stencil(masked_pad, field, fluid4):
    center = masked_pad[:, 1:-1, 1:-1]
    z_pad = jnp.pad(center, ((0, 0), (0, 0), (0, 0), (1, 1)))
    beside = masked_pad[:, 2:, 1:-1] + masked_pad[:, :-2, 1:-1]
    beside = beside + masked_pad[:, 1:-1, 2:] + masked_pad[:, 1:-1, :-2]
    beside = beside + z_pad[..., 2:] + z_pad[..., :-2]
    return fluid4 * (6.0 * field - beside) + (1.0 - fluid4) * field


def edges(masked):
    return extended(masked, (("gx", 1), ("gy", 2)), 1)


def gram(left, right):
    return jnp.einsum("rxyz,sxyz->rs", left, right, precision=lax.Precision.HIGHEST)


def combine(field, coeffs):
    return jnp.einsum("rxyz,rs->sxyz", field, coeffs, precision=lax.Precision.HIGHEST)


def solve_spd(matrix, rhs_mat):
    sym = 0.5 * (matrix + matrix.T)
    factor = jnp.linalg.cholesky(sym)
    inner = lax.linalg.triangular_solve(factor, rhs_mat, left_side=True, lower=True)
    return lax.linalg.triangular_solve(factor, inner, left_side=True, lower=True, transpose_a=True)


def shards(surface_tags, normal_index, fluid_mask, body_centers):
    cells_x, cells_y, depth_z = surface_tags.shape
    count_x = cells_x * lax.axis_size("gx")
    count_y = cells_y * lax.axis_size("gy")
    start_x = lax.axis_index("gx") * cells_x
    start_y = lax.axis_index("gy") * cells_y
    pos_z = (jnp.arange(depth_z).astype(jnp.float32) + 0.5) / depth_z
    fluid = fluid_mask.astype(jnp.float32)
    fluid4 = fluid[None]
    pos_x = ((start_x + jnp.arange(cells_x, dtype=jnp.int32)).astype(jnp.float32) + 0.5) / count_x
    pos_y = ((start_y + jnp.arange(cells_y, dtype=jnp.int32)).astype(jnp.float32) + 0.5) / count_y
    forcing = forcing_of(surface_tags, normal_index, fluid, body_centers, pos_x, pos_y, pos_z)
    rr0 = lax.psum(gram(forcing, forcing), ("gx", "gy"))
    q0 = stencil(edges(fluid4 * forcing), forcing, fluid4)
    pq0 = lax.psum(gram(forcing, q0), ("gx", "gy"))
    alpha0 = solve_spd(pq0, rr0)
    x1 = combine(forcing, alpha0)
    r1 = forcing - combine(q0, alpha0)
    rr1 = lax.psum(gram(r1, r1), ("gx", "gy"))
    beta = solve_spd(rr0, rr1)
    p1 = r1 + combine(forcing, beta)
    q1 = stencil(edges(fluid4 * p1), p1, fluid4)
    scale = 8.0 * BODIES / (count_x * count_y * depth_z)
    pq1 = lax.psum(gram(p1, q1), ("gx", "gy"))
    alpha1 = solve_spd(pq1, rr1)
    pressure = x1 + combine(p1, alpha1)
    added_mass = lax.psum(gram(forcing, pressure), ("gx", "gy")) * scale
    return (pressure, added_mass)


def solution(mesh):
    return jax.shard_map(
        shards,
        mesh=mesh,
        in_specs=(P("gx", "gy", None), P("gx", "gy", None), P("gx", "gy", None), P()),
        out_specs=(P(None, "gx", "gy", None), P()),
        check_vma=False,
    )
```

profile of v0, /device:TPU:1, one launch (start us, length us, event | category | flops | bytes accessed | tf_op | source)
XLA Modules:
  0.0 918.7 jit_solution(18269342550483081056)
XLA Ops:
  10.6 8.8 collective-permute-start
  19.4 3.3 collective-permute-start.1
  22.7 1.8 convolution_bitcast_fusion.3
  24.5 14.5 %collective-permute-done = f32[96,1,8,128]{3,0,2,1:T(8,128)S(1)} collective-permute-done((f32[96,1,8,128]{3,0,2,1:T(8,128)S(1)}, f32[96,1,8,128]{3,0,2,1:T(8,128)S(1)}, u32[]{:S(2)}, u32[]{:S(2)}) %collective-permute-start) | collective-permute-done | bytes 393248 | tf_op jit(solution)/shard_map/ppermute | solution.py:17
  39.0 1.3 collective-permute-start.2
  40.3 4.2 collective-permute-start.3
  44.5 0.9 collective-permute-done.2
  45.4 3.9 collective-permute-done.3
  49.9 1.6 convolution_bitcast_fusion.4
  51.4 451.5 %all-reduce.5.cloned.1.call-done = (f32[96,96]{1,0:T(8,128)}, f32[96,96]{1,0:T(8,128)}) async-done(((f32[96,96]{1,0:T(8,128)}, f32[96,96]{1,0:T(8,128)}), (f32[96,96]{1,0:T(8,128)}, f32[96,96]{1,0:T(8,128)})) %all-reduce.5.cloned.1.call-update) | async-done | bytes 73744 | tf_op jit(solution)/shard_map/psum | solution.py:92
  505.6 8.8 cholesky.70
  515.7 7.4 custom-call.15
  523.2 8.8 cholesky.59
  533.3 7.4 custom-call.13
  541.2 0.9 convolution_subtract_fusion
  543.0 102.1 %psum.37 = f32[96,96]{1,0:T(8,128)S(1)} all-reduce(f32[96,96]{1,0:T(8,128)S(1)} %convolution_bitcast_fusion.2), channel_id=1, replica_groups=mesh['gx'=32,'gy'=16] {'gx','gy'}, use_global_device_ids=true, to_apply=%region_4.8 | all-reduce | flops 9216 | bytes 73728 | tf_op jit(solution)/shard_map/psum | solution.py:98
  645.6 1.0 broadcast_multiply_fusion
  646.7 2.9 collective-permute-start.4
  649.5 6.6 collective-permute-start.5
  656.1 16.3 %collective-permute-done.4 = f32[96,1,8,128]{3,0,2,1:T(8,128)S(1)} collective-permute-done((f32[96,1,8,128]{3,0,2,1:T(8,128)S(1)}, f32[96,1,8,128]{3,0,2,1:T(8,128)S(1)}, u32[]{:S(2)}, u32[]{:S(2)}) %collective-permute-start.4) | collective-permute-done | bytes 393248 | tf_op jit(solution)/shard_map/ppermute | solution.py:17
  672.4 3.3 collective-permute-done.5
  675.8 1.3 collective-permute-start.6
  677.1 4.0 collective-permute-start.7
  681.1 1.0 fusion.27
  682.2 1.5 collective-permute-done.7
  683.6 1.2 convolution_bitcast_fusion.1
  684.9 104.7 %psum.38 = f32[96,96]{1,0:T(8,128)S(1)} all-reduce(f32[96,96]{1,0:T(8,128)S(1)} %convolution_bitcast_fusion.1), channel_id=1, replica_groups=mesh['gx'=32,'gy'=16] {'gx','gy'}, use_global_device_ids=true, to_apply=%region_5.9 | all-reduce | flops 9216 | bytes 73728 | tf_op jit(solution)/shard_map/psum | solution.py:103
  789.8 8.8 cholesky.81
  799.9 7.4 custom-call.17
  808.6 0.9 convolution_bitcast_fusion
  809.5 1.3 copy.33
  810.9 100.3 %psum.39 = f32[96,96]{1,0:T(8,128)S(1)} all-reduce(f32[96,96]{1,0:T(8,128)S(1)} %convolution_bitcast_fusion), channel_id=1, replica_groups=mesh['gx'=32,'gy'=16] {'gx','gy'}, use_global_device_ids=true, to_apply=%region_6.10 | all-reduce | flops 9216 | bytes 73728 | tf_op jit(solution)/shard_map/psum | solution.py:106
  (64 shorter events, 14.7 us)
Async XLA Ops:
  7.2 3.0 copy-start.1
  7.2 3.0 copy-start.2
  7.2 495.7 %all-reduce.5.cloned.1.call-start = ((), (), s32[]{:S(2)}) async-start(), calls=%async_computation | async-start | bytes 196608 | tf_op jit(solution)/shard_map/psum | solution.py:92
  10.6 28.4 %collective-permute-start = (f32[96,1,8,128]{3,0,2,1:T(8,128)S(1)}, f32[96,1,8,128]{3,0,2,1:T(8,128)S(1)}, u32[]{:S(2)}, u32[]{:S(2)}) collective-permute-start(f32[96,1,8,128]{3,0,2,1:T(8,128)S(1)} %get-tuple-element.20), channel_id=1, source_target_pairs={{16,0},{32,16},{48,32},{64,48},{80,64},{96,80},{112,96},{128,112},... | collective-permute-start | bytes 1179656 | tf_op jit(solution)/shard_map/ppermute | solution.py:17
  19.4 19.6 %collective-permute-start.1 = (f32[96,1,8,128]{3,0,2,1:T(8,128)S(1)}, f32[96,1,8,128]{3,0,2,1:T(8,128)S(1)}, u32[]{:S(2)}, u32[]{:S(2)}) collective-permute-start(f32[96,1,8,128]{3,0,2,1:T(8,128)S(1)} %get-tuple-element.19), channel_id=1, source_target_pairs={{0,16},{16,32},{32,48},{48,64},{64,80},{80,96},{96,112},{112,128},... | collective-permute-start | bytes 1179656 | tf_op jit(solution)/shard_map/ppermute | solution.py:16
  39.0 6.4 collective-permute-start.2
  40.3 9.0 collective-permute-start.3
  502.9 37.8 %copy-start = (f32[96,96]{1,0:T(8,128)S(1)}, f32[96,96]{1,0:T(8,128)}, u32[]{:S(2)}) copy-start(f32[96,96]{1,0:T(8,128)} %get-tuple-element.9) | copy-start | bytes 110596
  646.7 25.7 %collective-permute-start.4 = (f32[96,1,8,128]{3,0,2,1:T(8,128)S(1)}, f32[96,1,8,128]{3,0,2,1:T(8,128)S(1)}, u32[]{:S(2)}, u32[]{:S(2)}) collective-permute-start(f32[96,1,8,128]{3,0,2,1:T(8,128)S(1)} %get-tuple-element.18), channel_id=1, source_target_pairs={{16,0},{32,16},{48,32},{64,48},{80,64},{96,80},{112,96},{128,112},... | collective-permute-start | bytes 1179656 | tf_op jit(solution)/shard_map/ppermute | solution.py:17
  649.5 26.2 %collective-permute-start.5 = (f32[96,1,8,128]{3,0,2,1:T(8,128)S(1)}, f32[96,1,8,128]{3,0,2,1:T(8,128)S(1)}, u32[]{:S(2)}, u32[]{:S(2)}) collective-permute-start(f32[96,1,8,128]{3,0,2,1:T(8,128)S(1)} %get-tuple-element.17), channel_id=1, source_target_pairs={{0,16},{16,32},{32,48},{48,64},{64,80},{80,96},{96,112},{112,128},... | collective-permute-start | bytes 1179656 | tf_op jit(solution)/shard_map/ppermute | solution.py:16
  675.8 6.4 collective-permute-start.6
  677.1 6.6 collective-permute-start.7
Sparse Core Ops, SparseCore 0:
  51.6 451.2 all-reduce.4
where the time goes:
time: 920 us; the launch traced here: 919 us
  waiting for transfers between devices  492 us (53%)
  blocking collectives  307 us (33%)
  other arithmetic  56.8 us (6%)
  starting transfers between devices  32.4 us (4%)
  between operations  14.5 us (2%)
  matrix products  11.5 us (1%)
    psum x1, waiting for transfers between devices, shards(): rr0 = lax.psum(gram(forcing, forcing), ('gx', 'gy'))  451 us
    psum x1, blocking collectives, shards(): pq1 = lax.psum(gram(p1, q1), ('gx', 'gy'))  105 us
    psum x1, blocking collectives, shards(): rr1 = lax.psum(gram(r1, r1), ('gx', 'gy'))  102 us
    psum x1, blocking collectives, shards(): added_mass = lax.psum(gram(forcing, pressure), ('gx', 'gy')) * scale  100 us
    ppermute x4, waiting for transfers between devices, extended(): after = lax.ppermute(first, axis, down)  31.8 us
    another operation x9, other arithmetic, solve_spd(): factor = jnp.linalg.cholesky(sym)  28.4 us
    another operation x6, other arithmetic, solve_spd(): lax.linalg.triangular_solve(factor, inner, left_side=True, lower=True, tr...  24 us
  transfers between devices with their start and end apart: 9, of which 8 were waited for; matrix products, arithmetic and copies ran while one was open for 0% of the time, Pallas kernels for 0%

commit v1 on v0

v1 whole, which is shorter than its diff:
```python
import functools

import jax
import jax.numpy as jnp
import numpy as np
from jax import lax
from jax.experimental import pallas as pl
from jax.experimental.pallas import tpu as pltpu
from jax.sharding import Mesh, PartitionSpec as P

BODIES = 16
MODES = 6
COLS = BODIES * MODES
FOLD = 4 * MODES
GX = ("y", "zh", "c")
GY = ("x", "zl")
NEAR = ("y", "c", "x")
FAR = ("zh", "zl")
F32 = jnp.float32


def dot(left, right, dims):
    return lax.dot_general(
        left, right, (dims, ((), ())), precision=lax.Precision.HIGHEST, preferred_element_type=F32
    )


def mm(left, right):
    return dot(left, right, ((1,), (0,)))


def fields_kernel(nx, ny, nz, offs, ints, cen, lh, pay, rh, base, fext, qext, cx, cy):
    ex, ey = nx + 4, ny + 4
    tags, index, fluid = ints[0], ints[1], ints[2]
    shifted = index + (index >= 13).astype(jnp.int32)
    part_x = (shifted >= 9).astype(jnp.int32) + (shifted >= 18).astype(jnp.int32)
    rest = shifted - 9 * part_x
    part_y = (rest >= 3).astype(jnp.int32) + (rest >= 6).astype(jnp.int32)
    part_z = rest - 3 * part_y
    comps = [(part - 1).astype(F32) for part in (part_x, part_y, part_z)]
    square = comps[0] * comps[0] + comps[1] * comps[1] + comps[2] * comps[2]
    inverse = 1.0 / jnp.sqrt(square)
    fl = fluid.astype(F32)
    for m in range(3):
        base[m] = comps[m] * inverse * fl
    base[3] = fl
    base[4] = tags.astype(F32)

    col = lax.broadcasted_iota(jnp.int32, (COLS, nz), 0)
    body = (col * 43) >> 8
    mode = col - MODES * body
    bodyf = body.astype(F32)
    lane = lax.broadcasted_iota(jnp.int32, (COLS, nz), 1)
    one = [(mode == m).astype(F32) for m in range(MODES)]
    cen_x = jnp.broadcast_to(cen[:, 0:1], (COLS, nz))
    cen_y = jnp.broadcast_to(cen[:, 1:2], (COLS, nz))
    cen_z = jnp.broadcast_to(cen[:, 2:3], (COLS, nz))
    pos_z = (lane.astype(F32) + 0.5) * (1.0 / nz)
    lever_z = 3.0 * (pos_z - cen_z)
    start_x, start_y, count_x, count_y = offs[0], offs[1], offs[2], offs[3]
    coef_x0 = one[0] + one[4] * lever_z
    coef_y0 = one[1] - one[3] * lever_z
    for i in range(ex):
        pos = ((start_x + (i - 2)).astype(F32) + 0.5) / count_x.astype(F32)
        lever = 3.0 * (pos - cen_x)
        cx[0, i] = coef_y0 + one[5] * lever
        cx[1, i] = -one[4] * lever
    for j in range(ey):
        pos = ((start_y + (j - 2)).astype(F32) + 0.5) / count_y.astype(F32)
        lever = 3.0 * (pos - cen_y)
        cy[0, j] = coef_x0 - one[5] * lever
        cy[1, j] = one[2] + one[3] * lever

    def row(which, i, j):
        return jnp.broadcast_to(base[which, i, pl.ds(j, 1), :], (COLS, nz))

    def forcing_row(i, j):
        value = row(0, i, j) * cy[0, j] + row(1, i, j) * cx[0, i] + row(2, i, j) * (cy[1, j] + cx[1, i])
        fext[i, j] = jnp.where(row(4, i, j) == bodyf, value, 0.0)

    def operate(src, i, j):
        field = src[i, j]
        up = jnp.where(lane >= 1, pltpu.roll(field, 1, 1), 0.0)
        down = jnp.where(lane < nz - 1, pltpu.roll(field, nz - 1, 1), 0.0)
        beside = src[i + 1, j] + src[i - 1, j]
        beside = beside + src[i, j + 1] + src[i, j - 1]
        beside = beside + up + down
        return field + row(3, i, j) * (5.0 * field - beside)

    for i in range(ex):
        reach = 2 - max(2 - i, i - (nx + 1), 0)

        @pl.loop(2 - reach, ny + 2 + reach)
        def _(j, i=i):
            forcing_row(i, j)

    for i in range(1, ex - 1):
        reach = 1 - max(2 - i, i - (nx + 1), 0)

        @pl.loop(2 - reach, ny + 2 + reach)
        def _(j, i=i):
            qext[i, j] = operate(fext, i, j)

    for i in range(nx):

        @pl.loop(0, ny)
        def _(j, i=i):
            cells = pl.ds(pl.multiple_of((i * ny + j) * nz, nz), nz)
            forcing, field = fext[i + 2, j + 2], qext[i + 2, j + 2]
            lh[0:COLS, cells] = forcing
            lh[COLS : 2 * COLS, cells] = field
            rh[0:COLS, cells] = field
            rh[COLS : 2 * COLS, cells] = operate(qext, i + 2, j + 2)
            fold = forcing[0:FOLD]
            for k in range(1, COLS // FOLD):
                fold = fold + forcing[k * FOLD : (k + 1) * FOLD]
            rh[2 * COLS : 2 * COLS + FOLD, cells] = fold

    grams = dot(lh[...], rh[...], ((1,), (1,)))
    first, second = grams[0:COLS, 0:COLS], grams[COLS : 2 * COLS, 0:COLS]
    third = grams[COLS : 2 * COLS, COLS : 2 * COLS]
    zeroth = grams[0:COLS, 2 * COLS : 2 * COLS + FOLD]
    r = lax.broadcasted_iota(jnp.int32, (COLS, COLS), 0)
    c = lax.broadcasted_iota(jnp.int32, (COLS, COLS), 1)
    diagonal = jnp.sum(jnp.where(r == c, second, 0.0), axis=1, keepdims=True)
    pay[...] = jnp.zeros_like(pay)
    pay[0:COLS, 0:COLS] = jnp.where(r <= c, first, second)
    pay[0:COLS, COLS : COLS + FOLD] = zeroth
    pay[0:COLS, COLS + FOLD : COLS + FOLD + 1] = diagonal
    pay[COLS : 2 * COLS, 0:COLS] = third


def inverse_spd(matrix):
    size = matrix.shape[0]
    r8 = lax.broadcasted_iota(jnp.int32, (8, size), 0)
    lane = lax.broadcasted_iota(jnp.int32, (8, size), 1)
    blocks = [matrix[8 * b : 8 * b + 8] for b in range(size // 8)]
    for k in range(size):
        at, sub = k // 8, k % 8
        here = lane == k
        pivot_row = jnp.broadcast_to(blocks[at][sub : sub + 1, :], (8, size))
        pivot = jnp.broadcast_to(blocks[at][sub : sub + 1, k : k + 1], (8, size))
        recip = 1.0 / pivot
        scaled = jnp.where(here, recip, pivot_row * recip)
        new = []
        for b, block in enumerate(blocks):
            column = jnp.broadcast_to(block[:, k : k + 1], (8, size))
            kept = jnp.where(here, 0.0, block)
            if b == at:
                new.append(jnp.where(r8 == sub, scaled, kept - column * scaled))
            else:
                new.append(kept - column * scaled)
        blocks = new
    return jnp.concatenate(blocks, axis=0)


def solve_kernel(rows, nz, scale, pay, lh, out, added):
    r = lax.broadcasted_iota(jnp.int32, (COLS, COLS), 0)
    c = lax.broadcasted_iota(jnp.int32, (COLS, COLS), 1)
    both = pay[0:COLS, 0:COLS]
    both_t = both.T
    third = pay[COLS : 2 * COLS, 0:COLS]
    third = jnp.where(r <= c, third, third.T)
    first = jnp.where(r <= c, both, both_t)
    second = jnp.where(r > c, both, both_t)
    second = jnp.where(r == c, pay[0:COLS, COLS + FOLD : COLS + FOLD + 1], second)
    zeroth = pay[0:COLS, COLS : COLS + FOLD]
    zeroth = jnp.concatenate([zeroth] * (COLS // FOLD), axis=1)
    zeroth = jnp.where(((r * 43) >> 8) == ((c * 43) >> 8), zeroth, 0.0)
    first_inv = inverse_spd(first)
    left = mm(first_inv, second)
    right = mm(first_inv, zeroth)
    schur = third - mm(second, left)
    schur = 0.5 * (schur + schur.T)
    later = mm(inverse_spd(schur), first - mm(second, right))
    early = right - mm(left, later)
    added[...] = (mm(zeroth, early) + mm(first, later)) * scale
    coeffs = jnp.concatenate([early, later], axis=0)
    values = dot(coeffs, lh[...], ((0,), (0,)))
    for k in range(rows):
        out[pl.ds(k, COLS, stride=rows), :] = values[:, k * nz : (k + 1) * nz]


def halo(array, axis, dim, width):
    size, length = lax.axis_size(axis), array.shape[dim]
    up = [(i, i + 1) for i in range(size - 1)]
    down = [(j, i) for i, j in up]
    before = lax.ppermute(lax.slice_in_dim(array, length - width, length, axis=dim), axis, up)
    after = lax.ppermute(lax.slice_in_dim(array, 0, width, axis=dim), axis, down)
    return jnp.concatenate([before, array, after], axis=dim)


def reduced(part):
    near, far = (lax.axis_size(axes) for axes in (NEAR, FAR))
    rows, lanes = part.shape
    piece = lax.all_to_all(part, NEAR, 0, 0, tiled=True).reshape(near, rows // near, lanes).sum(0)
    piece = lax.all_to_all(jnp.broadcast_to(piece[None], (far,) + piece.shape), FAR, 0, 0, tiled=True).sum(0)
    return lax.all_to_all(
        jnp.broadcast_to(piece[None], (near,) + piece.shape), NEAR, 0, 0, tiled=True
    ).reshape(rows, lanes)


def shards(surface_tags, normal_index, fluid_mask, body_centers):
    nx, ny, nz = surface_tags.shape
    count_x = nx * lax.axis_size(GX)
    count_y = ny * lax.axis_size(GY)
    ints = jnp.stack([surface_tags, normal_index, fluid_mask])
    ints = halo(ints, GY, 2, 2)
    ints = halo(ints, GX, 1, 2)
    offs = jnp.stack(
        [
            lax.axis_index(GX) * nx,
            lax.axis_index(GY) * ny,
            jnp.int32(count_x),
            jnp.int32(count_y),
        ]
    ).astype(jnp.int32)
    cen = jnp.repeat(body_centers, MODES, axis=0)
    cells = nx * ny * nz
    vmem = pl.BlockSpec(memory_space=pltpu.VMEM)
    lh, pay = pl.pallas_call(
        functools.partial(fields_kernel, nx, ny, nz),
        out_shape=(
            jax.ShapeDtypeStruct((2 * COLS, cells), F32),
            jax.ShapeDtypeStruct((2 * COLS, 128), F32),
        ),
        in_specs=[pl.BlockSpec(memory_space=pltpu.SMEM), vmem, vmem],
        out_specs=(vmem, vmem),
        scratch_shapes=[
            pltpu.VMEM((2 * COLS + FOLD, cells), F32),
            pltpu.VMEM((5, nx + 4, ny + 4, nz), F32),
            pltpu.VMEM((nx + 4, ny + 4, COLS, nz), F32),
            pltpu.VMEM((nx + 4, ny + 4, COLS, nz), F32),
            pltpu.VMEM((2, nx + 4, COLS, nz), F32),
            pltpu.VMEM((2, ny + 4, COLS, nz), F32),
        ],
        compiler_params=pltpu.CompilerParams(vmem_limit_bytes=40 * 1024 * 1024),
        name="fields",
    )(offs, ints, cen)
    pay = reduced(pay)
    scale = 8.0 * BODIES / (count_x * count_y * nz)
    pressure, added = pl.pallas_call(
        functools.partial(solve_kernel, nx * ny, nz, scale),
        out_shape=(
            jax.ShapeDtypeStruct((COLS * nx * ny, nz), F32),
            jax.ShapeDtypeStruct((COLS, COLS), F32),
        ),
        in_specs=[vmem, vmem],
        out_specs=(vmem, vmem),
        compiler_params=pltpu.CompilerParams(vmem_limit_bytes=40 * 1024 * 1024),
        name="solve",
    )(pay, lh)
    return pressure.reshape(COLS, nx, ny, nz), added


def solution(mesh):
    split = Mesh(np.asarray(mesh.devices).reshape(4, 4, 2, 4, 4), GX + GY)
    return jax.shard_map(
        shards,
        mesh=split,
        in_specs=(P(GX, GY, None), P(GX, GY, None), P(GX, GY, None), P()),
        out_specs=(P(None, GX, GY, None), P()),
        check_vma=False,
    )
```

time: 920 us -> 119 us (0.13)
  waiting for transfers between devices: 492 us -> 3.36 us
  blocking collectives: 307 us -> 55.2 us
  other arithmetic: 56.8 us -> 2.42 us
  Pallas kernels: 0 us -> 37.9 us
  starting transfers between devices: 32.4 us -> 18.2 us
  between operations: 14.5 us -> 0.72 us
  matrix products: 11.5 us -> 0 us
    psum x1 -> x0, waiting for transfers between devices: 451 us -> none  [shards(): rr0 = lax.psum(gram(forcing, forcing), ('gx', 'gy'))]
    psum x3 -> x0, blocking collectives: 307 us -> none  [the longest x1 105 us: shards(): pq1 = lax.psum(gram(p1, q1), ('gx', 'gy'))]
    all_to_all x0 -> x3, blocking collectives: none -> 55.2 us  [the longest x1 25.5 us: reduced(): lax.all_to_all(part, NEAR, 0, 0, tiled=True)]
    another operation x16 -> x1, other arithmetic: 52.5 us -> 0.08 us  [shards(): jnp.stack([lax.axis_index(GX) * nx, lax.axis_index(GY) * ny, jnp.int32(co...]
    pallas_call x0 -> x2, Pallas kernels: none -> 37.9 us  [the longest x1 28.9 us: shards(): pl.pallas_call(functools.partial(solve_kernel, nx * ny, nz, scale), out_s...]
    ppermute x8 -> x4, waiting for transfers between devices: 40.5 us -> 3.36 us  [the longest x2 3.24 us: halo(): lax.ppermute(lax.slice_in_dim(array, 0, width, axis=dim), axis, down)]
    ppermute x8 -> x4, starting transfers between devices: 32.4 us -> 18.2 us  [the longest x2 10.2 us: halo(): lax.ppermute(lax.slice_in_dim(array, length - width, length, axis=dim), a...]
    dot_general x9 -> x0, matrix products: 9.96 us -> none  [the longest x5 6.23 us: gram(): jnp.einsum('rxyz,sxyz->rs', left, right, precision=lax.Precision.HIGHEST)]
  transfers between devices with their start and end apart: 9 -> 4, of which waited for: 8 -> 2; matrix products, arithmetic and copies ran while one was open for 0% -> 1% of each run, Pallas kernels for 0% -> 0%
where the time goes in v1:
time: 119 us
  blocking collectives  55.2 us (46%)
  Pallas kernels  37.9 us (32%)
  starting transfers between devices  18.2 us (15%)
  waiting for transfers between devices  3.36 us (3%)
  other arithmetic  2.42 us (2%)
    pallas_call x1, Pallas kernels, shards(): pl.pallas_call(functools.partial(solve_kernel, nx * ny, nz, scale), out_s...  28.9 us
    all_to_all x1, blocking collectives, reduced(): lax.all_to_all(part, NEAR, 0, 0, tiled=True)  25.5 us
    all_to_all x1, blocking collectives, reduced(): lax.all_to_all(jnp.broadcast_to(piece[None], (far,) + piece.shape), FAR,...  16.7 us
    all_to_all x1, blocking collectives, reduced(): lax.all_to_all(jnp.broadcast_to(piece[None], (near,) + piece.shape), NEAR...  12.9 us
    ppermute x2, starting transfers between devices, halo(): lax.ppermute(lax.slice_in_dim(array, length - width, length, axis=dim), a...  10.2 us
    pallas_call x1, Pallas kernels, shards(): pl.pallas_call(functools.partial(fields_kernel, nx, ny, nz), out_shape=(j...  9.07 us
    ppermute x2, starting transfers between devices, halo(): lax.ppermute(lax.slice_in_dim(array, 0, width, axis=dim), axis, down)  7.96 us
    ppermute x2, waiting for transfers between devices, halo(): lax.ppermute(lax.slice_in_dim(array, 0, width, axis=dim), axis, down)  3.24 us
  transfers between devices with their start and end apart: 4, of which 2 were waited for; matrix products, arithmetic and copies ran while one was open for 1% of the time, Pallas kernels for 0%

profile of v1, /device:TPU:1, one launch (start us, length us, event | category | flops | bytes accessed | tf_op | source)
XLA Modules:
  0.0 118.8 jit_solution(5408188017642422412)
XLA Ops:
  0.6 0.8 pad_add_fusion.4
  1.4 4.4 %collective-permute-start = (s32[3,2,2,128]{3,2,1,0:T(2,128)S(1)}, s32[3,2,2,128]{3,2,1,0:T(2,128)S(1)}, u32[]{:S(2)}, u32[]{:S(2)}) collective-permute-start(s32[3,2,2,128]{3,2,1,0:T(2,128)S(1)} %get-tuple-element.10), channel_id=1, source_target_pairs={{0,1},{1,2},{2,3},{3,4},{4,5},{5,6},{6,7},{7,8},{8,9},{9,10},{10,1... | collective-permute-start | bytes 18440 | tf_op jit(solution)/shard_map/ppermute | solution.py:188
  5.8 1.3 %collective-permute-start.1 = (s32[3,2,2,128]{3,2,1,0:T(2,128)S(1)}, s32[3,2,2,128]{3,2,1,0:T(2,128)S(1)}, u32[]{:S(2)}, u32[]{:S(2)}) collective-permute-start(s32[3,2,2,128]{3,2,1,0:T(2,128)S(1)} %get-tuple-element.11), channel_id=1, source_target_pairs={{1,0},{2,1},{3,2},{4,3},{5,4},{6,5},{7,6},{8,7},{9,8},{10,9},{11,1... | collective-permute-start | bytes 18440 | tf_op jit(solution)/shard_map/ppermute | solution.py:189
  7.1 0.0 collective-permute-done
  7.1 3.2 %collective-permute-done.1 = s32[3,2,2,128]{3,2,1,0:T(2,128)S(1)} collective-permute-done((s32[3,2,2,128]{3,2,1,0:T(2,128)S(1)}, s32[3,2,2,128]{3,2,1,0:T(2,128)S(1)}, u32[]{:S(2)}, u32[]{:S(2)}) %collective-permute-start.1) | collective-permute-done | bytes 6176 | tf_op jit(solution)/shard_map/ppermute | solution.py:189
  10.4 0.7 pad_add_fusion.1
  11.1 6.7 %collective-permute-start.3 = (s32[3,2,12,128]{3,2,1,0:T(8,128)S(1)}, s32[3,2,12,128]{3,2,1,0:T(8,128)S(1)}, u32[]{:S(2)}, u32[]{:S(2)}) collective-permute-start(s32[3,2,12,128]{3,2,1,0:T(8,128)S(1)} %pad_add_fusion.1), channel_id=1, source_target_pairs={{16,0},{32,16},{48,32},{64,48},{80,64},{96,80},{112,96},{128,112},... | collective-permute-start | bytes 110600 | tf_op jit(solution)/shard_map/ppermute | solution.py:189
  17.8 5.9 %collective-permute-start.2 = (s32[3,2,12,128]{3,2,1,0:T(8,128)S(1)}, s32[3,2,12,128]{3,2,1,0:T(8,128)S(1)}, u32[]{:S(2)}, u32[]{:S(2)}) collective-permute-start(s32[3,2,12,128]{3,2,1,0:T(8,128)S(1)} %pad_add_fusion.1), channel_id=1, source_target_pairs={{0,16},{16,32},{32,48},{48,64},{64,80},{80,96},{96,112},{112,128},... | collective-permute-start | bytes 110600 | tf_op jit(solution)/shard_map/ppermute | solution.py:188
  23.7 0.1 pad_add_fusion.5.offs
  23.7 0.8 broadcast_in_dim.6
  24.5 0.1 reshape.19
  24.6 0.1 copy.9.cen
  24.7 0.0 collective-permute-done.3
  24.7 0.1 collective-permute-done.2
  24.8 0.7 pad_add_fusion.ints
  25.6 9.1 %fields.1 = (f32[192,2048]{1,0:T(8,128)S(1)}, f32[192,128]{1,0:T(8,128)S(1)}) custom-call(s32[4]{0:T(128)S(1)} %pad_add_fusion.5.offs, s32[3,6,12,128]{3,2,1,0:T(8,128)S(1)} %pad_add_fusion.ints, f32[96,3]{1,0:T(8,128)S(1)} %copy.9.cen), custom_call_target="tpu_custom_call" | custom-call | tf_op jit(solution)/shard_map/fields/pallas_call | solution.py:221
  34.7 25.5 %all_to_all.19 = f32[32,6,128]{2,1,0:T(8,128)S(1)} all-to-all(f32[32,6,128]{2,1,0:T(8,128)S(1)} %all_to_all.12), channel_id=1, replica_groups=mesh['y'=4,'zh'=4,'c'=2,'x'=4,'zl'=4] {'y','c','x'}, dimensions={0} | all-to-all | bytes 196608 | tf_op jit(solution)/shard_map/all_to_all | solution.py:196
  60.2 16.7 %all_to_all.20 = f32[16,6,128]{2,1,0:T(8,128)S(1)} all-to-all(f32[16,6,128]{2,1,0:T(8,128)S(1)} %broadcast_in_dim.7), channel_id=1, replica_groups=mesh['y'=4,'zh'=4,'c'=2,'x'=4,'zl'=4] {'zh','zl'}, dimensions={0} | all-to-all | bytes 98304 | tf_op jit(solution)/shard_map/all_to_all | solution.py:197
  77.0 12.9 %all_to_all.21 = f32[32,6,128]{2,1,0:T(8,128)S(1)} all-to-all(f32[32,6,128]{2,1,0:T(8,128)S(1)} %broadcast_in_dim.8), channel_id=1, replica_groups=mesh['y'=4,'zh'=4,'c'=2,'x'=4,'zl'=4] {'y','c','x'}, dimensions={0} | all-to-all | bytes 196608 | tf_op jit(solution)/shard_map/all_to_all | solution.py:198
  89.9 28.9 %solve.1 = (f32[1536,128]{1,0:T(8,128)}, f32[96,96]{1,0:T(8,128)}) custom-call(f32[192,128]{1,0:T(8,128)S(1)} %reshape.20.pay, f32[192,2048]{1,0:T(8,128)S(1)} %get-tuple-element.7.lh), custom_call_target="tpu_custom_call" | custom-call | tf_op jit(solution)/shard_map/solve/pallas_call | solution.py:242
  (6 shorter events, 0.1 us)
Async XLA Ops:
  1.4 5.7 %collective-permute-start = (s32[3,2,2,128]{3,2,1,0:T(2,128)S(1)}, s32[3,2,2,128]{3,2,1,0:T(2,128)S(1)}, u32[]{:S(2)}, u32[]{:S(2)}) collective-permute-start(s32[3,2,2,128]{3,2,1,0:T(2,128)S(1)} %get-tuple-element.10), channel_id=1, source_target_pairs={{0,1},{1,2},{2,3},{3,4},{4,5},{5,6},{6,7},{7,8},{8,9},{9,10},{10,1... | collective-permute-start | bytes 18440 | tf_op jit(solution)/shard_map/ppermute | solution.py:188
  5.8 4.6 %collective-permute-start.1 = (s32[3,2,2,128]{3,2,1,0:T(2,128)S(1)}, s32[3,2,2,128]{3,2,1,0:T(2,128)S(1)}, u32[]{:S(2)}, u32[]{:S(2)}) collective-permute-start(s32[3,2,2,128]{3,2,1,0:T(2,128)S(1)} %get-tuple-element.11), channel_id=1, source_target_pairs={{1,0},{2,1},{3,2},{4,3},{5,4},{6,5},{7,6},{8,7},{9,8},{10,9},{11,1... | collective-permute-start | bytes 18440 | tf_op jit(solution)/shard_map/ppermute | solution.py:189
  11.1 13.6 %collective-permute-start.3 = (s32[3,2,12,128]{3,2,1,0:T(8,128)S(1)}, s32[3,2,12,128]{3,2,1,0:T(8,128)S(1)}, u32[]{:S(2)}, u32[]{:S(2)}) collective-permute-start(s32[3,2,12,128]{3,2,1,0:T(8,128)S(1)} %pad_add_fusion.1), channel_id=1, source_target_pairs={{16,0},{32,16},{48,32},{64,48},{80,64},{96,80},{112,96},{128,112},... | collective-permute-start | bytes 110600 | tf_op jit(solution)/shard_map/ppermute | solution.py:189
  17.8 7.0 %collective-permute-start.2 = (s32[3,2,12,128]{3,2,1,0:T(8,128)S(1)}, s32[3,2,12,128]{3,2,1,0:T(8,128)S(1)}, u32[]{:S(2)}, u32[]{:S(2)}) collective-permute-start(s32[3,2,12,128]{3,2,1,0:T(8,128)S(1)} %pad_add_fusion.1), channel_id=1, source_target_pairs={{0,16},{16,32},{32,48},{48,64},{64,80},{80,96},{96,112},{112,128},... | collective-permute-start | bytes 110600 | tf_op jit(solution)/shard_map/ppermute | solution.py:188

commit v2 on v1

--- a/solution.py
+++ b/solution.py
@@ -130,31 +130,37 @@
     pay[COLS : 2 * COLS, 0:COLS] = third
 
 
-def inverse_spd(matrix):
+def inverse_spd(matrix, work):
     size = matrix.shape[0]
-    r8 = lax.broadcasted_iota(jnp.int32, (8, size), 0)
-    lane = lax.broadcasted_iota(jnp.int32, (8, size), 1)
-    blocks = [matrix[8 * b : 8 * b + 8] for b in range(size // 8)]
-    for k in range(size):
-        at, sub = k // 8, k % 8
-        here = lane == k
-        pivot_row = jnp.broadcast_to(blocks[at][sub : sub + 1, :], (8, size))
-        pivot = jnp.broadcast_to(blocks[at][sub : sub + 1, k : k + 1], (8, size))
-        recip = 1.0 / pivot
-        scaled = jnp.where(here, recip, pivot_row * recip)
-        new = []
-        for b, block in enumerate(blocks):
-            column = jnp.broadcast_to(block[:, k : k + 1], (8, size))
-            kept = jnp.where(here, 0.0, block)
-            if b == at:
-                new.append(jnp.where(r8 == sub, scaled, kept - column * scaled))
-            else:
-                new.append(kept - column * scaled)
-        blocks = new
-    return jnp.concatenate(blocks, axis=0)
-
-
-def solve_kernel(rows, nz, scale, pay, lh, out, added):
+    r = lax.broadcasted_iota(jnp.int32, (size, size), 0)
+    c = lax.broadcasted_iota(jnp.int32, (size, size), 1)
+    diagonal = jnp.where(r == c, matrix, 0.0)
+    scale_r = lax.rsqrt(jnp.sum(diagonal, axis=1, keepdims=True))
+    scale_c = lax.rsqrt(jnp.sum(diagonal, axis=0, keepdims=True))
+    scaled = matrix * scale_r * scale_c
+    bound = jnp.max(jnp.sum(jnp.abs(scaled), axis=0, keepdims=True), axis=1, keepdims=True)
+    weight = jnp.minimum(1.0, 1.9 / bound)
+    eye = (r == c).astype(F32)
+    rest = eye - weight * scaled
+    work[0:size] = eye + rest
+    work[size : 2 * size] = rest
+
+    def longer(carry):
+        power = work[size : 2 * size]
+        spread = jnp.sum(power * power)
+        total = work[0:size]
+        power = mm(power, power)
+        total = total + mm(total, power)
+        power = mm(power, power)
+        work[0:size] = total + mm(total, power)
+        work[size : 2 * size] = power
+        return carry[0] + 1, spread > 1e-4
+
+    lax.while_loop(lambda carry: (carry[0] < 14) & carry[1], longer, (jnp.int32(0), jnp.bool_(True)))
+    return work[0:size] * (weight * scale_r) * scale_c
+
+
+def solve_kernel(rows, nz, scale, pay, lh, out, added, work):
     r = lax.broadcasted_iota(jnp.int32, (COLS, COLS), 0)
     c = lax.broadcasted_iota(jnp.int32, (COLS, COLS), 1)
     both = pay[0:COLS, 0:COLS]
@@ -167,16 +173,16 @@
     zeroth = pay[0:COLS, COLS : COLS + FOLD]
     zeroth = jnp.concatenate([zeroth] * (COLS // FOLD), axis=1)
     zeroth = jnp.where(((r * 43) >> 8) == ((c * 43) >> 8), zeroth, 0.0)
-    first_inv = inverse_spd(first)
+    first_inv = inverse_spd(first, work)
     left = mm(first_inv, second)
     right = mm(first_inv, zeroth)
     schur = third - mm(second, left)
     schur = 0.5 * (schur + schur.T)
-    later = mm(inverse_spd(schur), first - mm(second, right))
+    later = mm(inverse_spd(schur, work), first - mm(second, right))
     early = right - mm(left, later)
-    added[...] = (mm(zeroth, early) + mm(first, later)) * scale
     coeffs = jnp.concatenate([early, later], axis=0)
     values = dot(coeffs, lh[...], ((0,), (0,)))
+    added[...] = (mm(zeroth, early) + mm(first, later)) * scale
     for k in range(rows):
         out[pl.ds(k, COLS, stride=rows), :] = values[:, k * nz : (k + 1) * nz]
 
@@ -247,6 +253,7 @@
         ),
         in_specs=[vmem, vmem],
         out_specs=(vmem, vmem),
+        scratch_shapes=[pltpu.VMEM((2 * COLS, COLS), F32)],
         compiler_params=pltpu.CompilerParams(vmem_limit_bytes=40 * 1024 * 1024),
         name="solve",
     )(pay, lh)

time: 119 us -> 99 us (0.83)
  Pallas kernels: 37.9 us -> 17.5 us
    pallas_call x1, Pallas kernels: 28.9 us -> 8.42 us  [shards(): pl.pallas_call(functools.partial(solve_kernel, nx * ny, nz, scale), out_s...]
where the time goes in v2:
time: 99 us; the launch traced here: 98.4 us
  blocking collectives  55.2 us (56%)
  starting transfers between devices  18.2 us (18%)
  Pallas kernels  17.5 us (18%)
  waiting for transfers between devices  3.36 us (3%)
  other arithmetic  2.41 us (2%)
  local copies, waits for them, and re-layouts  1.02 us (1%)
    all_to_all x1, blocking collectives, reduced(): lax.all_to_all(part, NEAR, 0, 0, tiled=True)  25.5 us
    all_to_all x1, blocking collectives, reduced(): lax.all_to_all(jnp.broadcast_to(piece[None], (far,) + piece.shape), FAR,...  16.7 us
    all_to_all x1, blocking collectives, reduced(): lax.all_to_all(jnp.broadcast_to(piece[None], (near,) + piece.shape), NEAR...  12.9 us
    ppermute x2, starting transfers between devices, halo(): lax.ppermute(lax.slice_in_dim(array, length - width, length, axis=dim), a...  10.2 us
    pallas_call x1, Pallas kernels, shards(): pl.pallas_call(functools.partial(fields_kernel, nx, ny, nz), out_shape=(j...  9.07 us
    pallas_call x1, Pallas kernels, shards(): pl.pallas_call(functools.partial(solve_kernel, nx * ny, nz, scale), out_s...  8.42 us
    ppermute x2, starting transfers between devices, halo(): lax.ppermute(lax.slice_in_dim(array, 0, width, axis=dim), axis, down)  7.96 us
    ppermute x2, waiting for transfers between devices, halo(): lax.ppermute(lax.slice_in_dim(array, 0, width, axis=dim), axis, down)  3.24 us
  transfers between devices with their start and end apart: 4, of which 2 were waited for; matrix products, arithmetic and copies ran while one was open for 1% of the time, Pallas kernels for 0%

profile of v2, /device:TPU:1, one launch (start us, length us, event | category | flops | bytes accessed | tf_op | source)
XLA Modules:
  0.0 98.4 jit_solution(8591366565919968997)
XLA Ops:
  0.6 0.8 pad_add_fusion.4
  1.4 4.4 %collective-permute-start = (s32[3,2,2,128]{3,2,1,0:T(2,128)S(1)}, s32[3,2,2,128]{3,2,1,0:T(2,128)S(1)}, u32[]{:S(2)}, u32[]{:S(2)}) collective-permute-start(s32[3,2,2,128]{3,2,1,0:T(2,128)S(1)} %get-tuple-element.10), channel_id=1, source_target_pairs={{0,1},{1,2},{2,3},{3,4},{4,5},{5,6},{6,7},{7,8},{8,9},{9,10},{10,1... | collective-permute-start | bytes 18440 | tf_op jit(solution)/shard_map/ppermute | solution.py:194
  5.8 1.3 %collective-permute-start.1 = (s32[3,2,2,128]{3,2,1,0:T(2,128)S(1)}, s32[3,2,2,128]{3,2,1,0:T(2,128)S(1)}, u32[]{:S(2)}, u32[]{:S(2)}) collective-permute-start(s32[3,2,2,128]{3,2,1,0:T(2,128)S(1)} %get-tuple-element.11), channel_id=1, source_target_pairs={{1,0},{2,1},{3,2},{4,3},{5,4},{6,5},{7,6},{8,7},{9,8},{10,9},{11,1... | collective-permute-start | bytes 18440 | tf_op jit(solution)/shard_map/ppermute | solution.py:195
  7.1 0.0 collective-permute-done
  7.1 3.2 %collective-permute-done.1 = s32[3,2,2,128]{3,2,1,0:T(2,128)S(1)} collective-permute-done((s32[3,2,2,128]{3,2,1,0:T(2,128)S(1)}, s32[3,2,2,128]{3,2,1,0:T(2,128)S(1)}, u32[]{:S(2)}, u32[]{:S(2)}) %collective-permute-start.1) | collective-permute-done | bytes 6176 | tf_op jit(solution)/shard_map/ppermute | solution.py:195
  10.4 0.7 pad_add_fusion.1
  11.1 6.7 %collective-permute-start.3 = (s32[3,2,12,128]{3,2,1,0:T(8,128)S(1)}, s32[3,2,12,128]{3,2,1,0:T(8,128)S(1)}, u32[]{:S(2)}, u32[]{:S(2)}) collective-permute-start(s32[3,2,12,128]{3,2,1,0:T(8,128)S(1)} %pad_add_fusion.1), channel_id=1, source_target_pairs={{16,0},{32,16},{48,32},{64,48},{80,64},{96,80},{112,96},{128,112},... | collective-permute-start | bytes 110600 | tf_op jit(solution)/shard_map/ppermute | solution.py:195
  17.8 5.9 %collective-permute-start.2 = (s32[3,2,12,128]{3,2,1,0:T(8,128)S(1)}, s32[3,2,12,128]{3,2,1,0:T(8,128)S(1)}, u32[]{:S(2)}, u32[]{:S(2)}) collective-permute-start(s32[3,2,12,128]{3,2,1,0:T(8,128)S(1)} %pad_add_fusion.1), channel_id=1, source_target_pairs={{0,16},{16,32},{32,48},{48,64},{64,80},{80,96},{96,112},{112,128},... | collective-permute-start | bytes 110600 | tf_op jit(solution)/shard_map/ppermute | solution.py:194
  23.7 0.1 pad_add_fusion.5.offs
  23.7 0.8 broadcast_in_dim.6
  24.5 0.1 reshape.19
  24.6 0.1 copy.9.cen
  24.7 0.0 collective-permute-done.3
  24.7 0.1 collective-permute-done.2
  24.8 0.7 pad_add_fusion.ints
  25.6 9.1 %fields.1 = (f32[192,2048]{1,0:T(8,128)S(1)}, f32[192,128]{1,0:T(8,128)S(1)}) custom-call(s32[4]{0:T(128)S(1)} %pad_add_fusion.5.offs, s32[3,6,12,128]{3,2,1,0:T(8,128)S(1)} %pad_add_fusion.ints, f32[96,3]{1,0:T(8,128)S(1)} %copy.9.cen), custom_call_target="tpu_custom_call" | custom-call | tf_op jit(solution)/shard_map/fields/pallas_call | solution.py:227
  34.7 25.5 %all_to_all.19 = f32[32,6,128]{2,1,0:T(8,128)S(1)} all-to-all(f32[32,6,128]{2,1,0:T(8,128)S(1)} %all_to_all.12), channel_id=1, replica_groups=mesh['y'=4,'zh'=4,'c'=2,'x'=4,'zl'=4] {'y','c','x'}, dimensions={0} | all-to-all | bytes 196608 | tf_op jit(solution)/shard_map/all_to_all | solution.py:202
  60.2 16.7 %all_to_all.20 = f32[16,6,128]{2,1,0:T(8,128)S(1)} all-to-all(f32[16,6,128]{2,1,0:T(8,128)S(1)} %broadcast_in_dim.7), channel_id=1, replica_groups=mesh['y'=4,'zh'=4,'c'=2,'x'=4,'zl'=4] {'zh','zl'}, dimensions={0} | all-to-all | bytes 98304 | tf_op jit(solution)/shard_map/all_to_all | solution.py:203
  77.0 12.9 %all_to_all.21 = f32[32,6,128]{2,1,0:T(8,128)S(1)} all-to-all(f32[32,6,128]{2,1,0:T(8,128)S(1)} %broadcast_in_dim.8), channel_id=1, replica_groups=mesh['y'=4,'zh'=4,'c'=2,'x'=4,'zl'=4] {'y','c','x'}, dimensions={0} | all-to-all | bytes 196608 | tf_op jit(solution)/shard_map/all_to_all | solution.py:204
  89.9 8.4 %solve.1 = (f32[1536,128]{1,0:T(8,128)}, f32[96,96]{1,0:T(8,128)}) custom-call(f32[192,128]{1,0:T(8,128)S(1)} %reshape.20.pay, f32[192,2048]{1,0:T(8,128)S(1)} %get-tuple-element.7.lh), custom_call_target="tpu_custom_call" | custom-call | tf_op jit(solution)/shard_map/solve/pallas_call | solution.py:248
  (6 shorter events, 0.1 us)
Async XLA Ops:
  1.4 5.7 %collective-permute-start = (s32[3,2,2,128]{3,2,1,0:T(2,128)S(1)}, s32[3,2,2,128]{3,2,1,0:T(2,128)S(1)}, u32[]{:S(2)}, u32[]{:S(2)}) collective-permute-start(s32[3,2,2,128]{3,2,1,0:T(2,128)S(1)} %get-tuple-element.10), channel_id=1, source_target_pairs={{0,1},{1,2},{2,3},{3,4},{4,5},{5,6},{6,7},{7,8},{8,9},{9,10},{10,1... | collective-permute-start | bytes 18440 | tf_op jit(solution)/shard_map/ppermute | solution.py:194
  5.8 4.6 %collective-permute-start.1 = (s32[3,2,2,128]{3,2,1,0:T(2,128)S(1)}, s32[3,2,2,128]{3,2,1,0:T(2,128)S(1)}, u32[]{:S(2)}, u32[]{:S(2)}) collective-permute-start(s32[3,2,2,128]{3,2,1,0:T(2,128)S(1)} %get-tuple-element.11), channel_id=1, source_target_pairs={{1,0},{2,1},{3,2},{4,3},{5,4},{6,5},{7,6},{8,7},{9,8},{10,9},{11,1... | collective-permute-start | bytes 18440 | tf_op jit(solution)/shard_map/ppermute | solution.py:195
  11.1 13.6 %collective-permute-start.3 = (s32[3,2,12,128]{3,2,1,0:T(8,128)S(1)}, s32[3,2,12,128]{3,2,1,0:T(8,128)S(1)}, u32[]{:S(2)}, u32[]{:S(2)}) collective-permute-start(s32[3,2,12,128]{3,2,1,0:T(8,128)S(1)} %pad_add_fusion.1), channel_id=1, source_target_pairs={{16,0},{32,16},{48,32},{64,48},{80,64},{96,80},{112,96},{128,112},... | collective-permute-start | bytes 110600 | tf_op jit(solution)/shard_map/ppermute | solution.py:195
  17.8 7.0 %collective-permute-start.2 = (s32[3,2,12,128]{3,2,1,0:T(8,128)S(1)}, s32[3,2,12,128]{3,2,1,0:T(8,128)S(1)}, u32[]{:S(2)}, u32[]{:S(2)}) collective-permute-start(s32[3,2,12,128]{3,2,1,0:T(8,128)S(1)} %pad_add_fusion.1), channel_id=1, source_target_pairs={{0,16},{16,32},{32,48},{48,64},{64,80},{80,96},{96,112},{112,128},... | collective-permute-start | bytes 110600 | tf_op jit(solution)/shard_map/ppermute | solution.py:194

commit v3 on v2

--- a/solution.py
+++ b/solution.py
@@ -29,22 +29,50 @@
     return dot(left, right, ((1,), (0,)))
 
 
-def fields_kernel(nx, ny, nz, offs, ints, cen, lh, pay, rh, base, fext, qext, cx, cy):
+def fields_kernel(nx, ny, nz, info, own, pair, across, even, odd, cen, lh, pay, rh, base, fext, qext, cx, cy):
     ex, ey = nx + 4, ny + 4
-    tags, index, fluid = ints[0], ints[1], ints[2]
-    shifted = index + (index >= 13).astype(jnp.int32)
-    part_x = (shifted >= 9).astype(jnp.int32) + (shifted >= 18).astype(jnp.int32)
-    rest = shifted - 9 * part_x
-    part_y = (rest >= 3).astype(jnp.int32) + (rest >= 6).astype(jnp.int32)
-    part_z = rest - 3 * part_y
-    comps = [(part - 1).astype(F32) for part in (part_x, part_y, part_z)]
-    square = comps[0] * comps[0] + comps[1] * comps[1] + comps[2] * comps[2]
-    inverse = 1.0 / jnp.sqrt(square)
-    fl = fluid.astype(F32)
-    for m in range(3):
-        base[m] = comps[m] * inverse * fl
-    base[3] = fl
-    base[4] = tags.astype(F32)
+    start_x, start_y, count_x, count_y, core, parity = (info[k] for k in range(6))
+    first_core = core == 0
+    above_is_even = parity == 0
+    dense_lane = lax.broadcasted_iota(jnp.int32, (1, nz), 1)
+
+    def describe(cells, layers, rows, shifts):
+        tags, index, fluid = cells
+        shifted = index + (index >= 13).astype(jnp.int32)
+        part_x = (shifted >= 9).astype(jnp.int32) + (shifted >= 18).astype(jnp.int32)
+        rest = shifted - 9 * part_x
+        part_y = (rest >= 3).astype(jnp.int32) + (rest >= 6).astype(jnp.int32)
+        part_z = rest - 3 * part_y
+        comps = [(part - 1).astype(F32) for part in (part_x, part_y, part_z)]
+        inverse = 1.0 / jnp.sqrt(comps[0] * comps[0] + comps[1] * comps[1] + comps[2] * comps[2])
+        fl = fluid.astype(F32)
+        values = [comp * inverse * fl for comp in comps] + [tags.astype(F32)]
+        for m, value in enumerate(values):
+            base[m, layers, rows] = value
+            if shifts:
+                after = pltpu.roll(value, nz - 1, value.ndim - 1)
+                before = pltpu.roll(value, 1, value.ndim - 1)
+                if m == 3:
+                    after = jnp.where(dense_lane == nz - 1, -1.0, after)
+                    before = jnp.where(dense_lane == 0, -1.0, before)
+                base[4 + m, layers, rows] = after
+                base[8 + m, layers, rows] = before
+        base[12, layers, rows] = fl
+
+    mine = pl.ds(0, ny)
+    other = pair[1 - core]
+    beyond = across[...]
+    before = jnp.where(first_core, beyond, other)
+    after = jnp.where(first_core, other, beyond)
+    for layer in range(nx):
+        describe([before[k, layer] for k in range(3)], layer, mine, layer == nx - 1)
+        describe([own[k, layer] for k in range(3)], layer + 2, mine, True)
+        describe([after[k, layer] for k in range(3)], layer + 2 + nx, mine, layer == 0)
+    above = jnp.where(above_is_even, even[...], odd[...])
+    below = jnp.where(above_is_even, odd[...], even[...])
+    for layer in range(nx + 2):
+        describe([above[k, layer] for k in range(3)], layer + 1, pl.ds(ny, 2), True)
+        describe([below[k, layer] for k in range(3)], layer + 1, pl.ds(ny + 2, 2), True)
 
     col = lax.broadcasted_iota(jnp.int32, (COLS, nz), 0)
     body = (col * 43) >> 8
@@ -57,7 +85,8 @@
     cen_z = jnp.broadcast_to(cen[:, 2:3], (COLS, nz))
     pos_z = (lane.astype(F32) + 0.5) * (1.0 / nz)
     lever_z = 3.0 * (pos_z - cen_z)
-    start_x, start_y, count_x, count_y = offs[0], offs[1], offs[2], offs[3]
+    step3 = one[3] * (3.0 / nz)
+    step4 = one[4] * (3.0 / nz)
     coef_x0 = one[0] + one[4] * lever_z
     coef_y0 = one[1] - one[3] * lever_z
     for i in range(ex):
@@ -66,51 +95,58 @@
         cx[0, i] = coef_y0 + one[5] * lever
         cx[1, i] = -one[4] * lever
     for j in range(ey):
-        pos = ((start_y + (j - 2)).astype(F32) + 0.5) / count_y.astype(F32)
+        pos = ((start_y + (j if j < ny + 2 else j - ey)).astype(F32) + 0.5) / count_y.astype(F32)
         lever = 3.0 * (pos - cen_y)
         cy[0, j] = coef_x0 - one[5] * lever
         cy[1, j] = one[2] + one[3] * lever
 
+    def at(j):
+        return jnp.where(j < 0, j + ey, jnp.where(j >= ey, j - ey, j))
+
     def row(which, i, j):
         return jnp.broadcast_to(base[which, i, pl.ds(j, 1), :], (COLS, nz))
 
-    def forcing_row(i, j):
-        value = row(0, i, j) * cy[0, j] + row(1, i, j) * cx[0, i] + row(2, i, j) * (cy[1, j] + cx[1, i])
-        fext[i, j] = jnp.where(row(4, i, j) == bodyf, value, 0.0)
-
-    def operate(src, i, j):
-        field = src[i, j]
-        up = jnp.where(lane >= 1, pltpu.roll(field, 1, 1), 0.0)
-        down = jnp.where(lane < nz - 1, pltpu.roll(field, nz - 1, 1), 0.0)
+    def forcing_row(first, i, j, coef_x, coef_y, coef_z):
+        value = row(first, i, j) * coef_x + row(first + 1, i, j) * coef_y + row(first + 2, i, j) * coef_z
+        return jnp.where(row(first + 3, i, j) == bodyf, value, 0.0)
+
+    def apply(src, i, j, field, along_z):
         beside = src[i + 1, j] + src[i - 1, j]
-        beside = beside + src[i, j + 1] + src[i, j - 1]
-        beside = beside + up + down
-        return field + row(3, i, j) * (5.0 * field - beside)
+        beside = beside + src[i, at(j + 1)] + src[i, at(j - 1)]
+        beside = beside + along_z
+        return field + row(12, i, j) * (5.0 * field - beside)
 
     for i in range(ex):
         reach = 2 - max(2 - i, i - (nx + 1), 0)
 
-        @pl.loop(2 - reach, ny + 2 + reach)
+        @pl.loop(-reach, ny + reach)
         def _(j, i=i):
-            forcing_row(i, j)
+            j = at(j)
+            fext[i, j] = forcing_row(0, i, j, cy[0, j], cx[0, i], cy[1, j] + cx[1, i])
 
     for i in range(1, ex - 1):
         reach = 1 - max(2 - i, i - (nx + 1), 0)
 
-        @pl.loop(2 - reach, ny + 2 + reach)
+        @pl.loop(-reach, ny + reach)
         def _(j, i=i):
-            qext[i, j] = operate(fext, i, j)
-
-    for i in range(nx):
-
-        @pl.loop(0, ny)
+            j = at(j)
+            coef_x, coef_y, coef_z = cy[0, j], cx[0, i], cy[1, j] + cx[1, i]
+            along_z = forcing_row(4, i, j, coef_x + step4, coef_y - step3, coef_z)
+            along_z = along_z + forcing_row(8, i, j, coef_x - step4, coef_y + step3, coef_z)
+            qext[i, j] = apply(fext, i, j, fext[i, j], along_z)
+
+    for i in range(2, nx + 2):
+
+        @pl.loop(0, ny, unroll=8)
         def _(j, i=i):
-            cells = pl.ds(pl.multiple_of((i * ny + j) * nz, nz), nz)
-            forcing, field = fext[i + 2, j + 2], qext[i + 2, j + 2]
+            cells = pl.ds(pl.multiple_of(((i - 2) * ny + j) * nz, nz), nz)
+            forcing, field = fext[i, j], qext[i, j]
+            up = jnp.where(lane >= 1, pltpu.roll(field, 1, 1), 0.0)
+            down = jnp.where(lane < nz - 1, pltpu.roll(field, nz - 1, 1), 0.0)
             lh[0:COLS, cells] = forcing
             lh[COLS : 2 * COLS, cells] = field
             rh[0:COLS, cells] = field
-            rh[COLS : 2 * COLS, cells] = operate(qext, i + 2, j + 2)
+            rh[COLS : 2 * COLS, cells] = apply(qext, i, j, field, up + down)
             fold = forcing[0:FOLD]
             for k in range(1, COLS // FOLD):
                 fold = fold + forcing[k * FOLD : (k + 1) * FOLD]
@@ -187,13 +223,10 @@
         out[pl.ds(k, COLS, stride=rows), :] = values[:, k * nz : (k + 1) * nz]
 
 
-def halo(array, axis, dim, width):
-    size, length = lax.axis_size(axis), array.shape[dim]
-    up = [(i, i + 1) for i in range(size - 1)]
-    down = [(j, i) for i, j in up]
-    before = lax.ppermute(lax.slice_in_dim(array, length - width, length, axis=dim), axis, up)
-    after = lax.ppermute(lax.slice_in_dim(array, 0, width, axis=dim), axis, down)
-    return jnp.concatenate([before, array, after], axis=dim)
+def swap(array, axes, start):
+    size = lax.axis_size(axes)
+    pairs = [(i, i + 1) for i in range(start, size - 1, 2)]
+    return lax.ppermute(array, axes, pairs + [(j, i) for i, j in pairs])
 
 
 def reduced(part):
@@ -210,16 +243,19 @@
     nx, ny, nz = surface_tags.shape
     count_x = nx * lax.axis_size(GX)
     count_y = ny * lax.axis_size(GY)
-    ints = jnp.stack([surface_tags, normal_index, fluid_mask])
-    ints = halo(ints, GY, 2, 2)
-    ints = halo(ints, GX, 1, 2)
-    offs = jnp.stack(
-        [
-            lax.axis_index(GX) * nx,
-            lax.axis_index(GY) * ny,
-            jnp.int32(count_x),
-            jnp.int32(count_y),
-        ]
+    at_x, at_y, core = lax.axis_index(GX), lax.axis_index(GY), lax.axis_index("c")
+    own = jnp.stack([surface_tags, normal_index, fluid_mask])
+    across = swap(own, GX, 1)
+    pair = lax.all_gather(own, "c")
+    before = jnp.where(core == 0, across, pair[0])[:, nx - 1 :]
+    after = jnp.where(core == 0, pair[1], across)[:, :1]
+    near = jnp.concatenate([before, own, after], axis=1)
+    first, last = near[:, :, :2], near[:, :, ny - 2 :]
+    parity = at_y % 2
+    odd = swap(jnp.where(parity == 0, first, last), GY, 1)
+    even = swap(jnp.where(parity == 0, last, first), GY, 0)
+    info = jnp.stack(
+        [at_x * nx, at_y * ny, jnp.int32(count_x), jnp.int32(count_y), core, parity]
     ).astype(jnp.int32)
     cen = jnp.repeat(body_centers, MODES, axis=0)
     cells = nx * ny * nz
@@ -230,11 +266,11 @@
             jax.ShapeDtypeStruct((2 * COLS, cells), F32),
             jax.ShapeDtypeStruct((2 * COLS, 128), F32),
         ),
-        in_specs=[pl.BlockSpec(memory_space=pltpu.SMEM), vmem, vmem],
+        in_specs=[pl.BlockSpec(memory_space=pltpu.SMEM)] + [vmem] * 6,
         out_specs=(vmem, vmem),
         scratch_shapes=[
             pltpu.VMEM((2 * COLS + FOLD, cells), F32),
-            pltpu.VMEM((5, nx + 4, ny + 4, nz), F32),
+            pltpu.VMEM((13, nx + 4, ny + 4, nz), F32),
             pltpu.VMEM((nx + 4, ny + 4, COLS, nz), F32),
             pltpu.VMEM((nx + 4, ny + 4, COLS, nz), F32),
             pltpu.VMEM((2, nx + 4, COLS, nz), F32),
@@ -242,7 +278,7 @@
         ],
         compiler_params=pltpu.CompilerParams(vmem_limit_bytes=40 * 1024 * 1024),
         name="fields",
-    )(offs, ints, cen)
+    )(info, own, pair, across, even, odd, cen)
     pay = reduced(pay)
     scale = 8.0 * BODIES / (count_x * count_y * nz)
     pressure, added = pl.pallas_call(

time: 99 us -> 93.8 us (0.947)
  blocking collectives: 55.2 us -> 60.5 us
  starting transfers between devices: 18.2 us -> 14.4 us
  waiting for transfers between devices: 3.36 us -> 0.01 us
  Pallas kernels: 17.5 us -> 14.9 us
    all_to_all x1, blocking collectives: 16.7 us -> 21.8 us  [reduced(): lax.all_to_all(jnp.broadcast_to(piece[None], (far,) + piece.shape), FAR,...]
    ppermute x4 -> x3, starting transfers between devices: 18.2 us -> 14.4 us  [swap(): return lax.ppermute(array, axes, pairs + [(j, i) for i, j in pairs])]
    ppermute x4 -> x3, waiting for transfers between devices: 3.36 us -> 0.01 us  [swap(): return lax.ppermute(array, axes, pairs + [(j, i) for i, j in pairs])]
    pallas_call x1, Pallas kernels: 9.07 us -> 6.47 us  [shards(): pl.pallas_call(functools.partial(fields_kernel, nx, ny, nz), out_shape=(j...]
    all_gather x0 -> x1, blocking collectives: none -> 1.84 us  [shards(): pair = lax.all_gather(own, 'c')]
    all_to_all x1, blocking collectives: 25.5 us -> 23.9 us  [reduced(): lax.all_to_all(part, NEAR, 0, 0, tiled=True)]
    concatenate x2 -> x0, other arithmetic: 1.49 us -> none  [halo(): return jnp.concatenate([before, array, after], axis=dim)]
  transfers between devices with their start and end apart: 4 -> 3, of which waited for: 2 -> 0; matrix products, arithmetic and copies ran while one was open for 1% -> 1% of each run, Pallas kernels for 0% -> 0%
where the time goes in v3:
time: 93.8 us; the launch traced here: 93.2 us
  blocking collectives  60.5 us (64%)
  Pallas kernels  14.9 us (16%)
  starting transfers between devices  14.4 us (15%)
  other arithmetic  1.6 us (2%)
  local copies, waits for them, and re-layouts  1.11 us (1%)
    all_to_all x1, blocking collectives, reduced(): lax.all_to_all(part, NEAR, 0, 0, tiled=True)  23.9 us
    all_to_all x1, blocking collectives, reduced(): lax.all_to_all(jnp.broadcast_to(piece[None], (far,) + piece.shape), FAR,...  21.8 us
    ppermute x3, starting transfers between devices, swap(): return lax.ppermute(array, axes, pairs + [(j, i) for i, j in pairs])  14.4 us
    all_to_all x1, blocking collectives, reduced(): lax.all_to_all(jnp.broadcast_to(piece[None], (near,) + piece.shape), NEAR...  12.9 us
    pallas_call x1, Pallas kernels, shards(): pl.pallas_call(functools.partial(solve_kernel, nx * ny, nz, scale), out_s...  8.42 us
    pallas_call x1, Pallas kernels, shards(): pl.pallas_call(functools.partial(fields_kernel, nx, ny, nz), out_shape=(j...  6.47 us
  transfers between devices with their start and end apart: 3, of which 0 were waited for; matrix products, arithmetic and copies ran while one was open for 1% of the time, Pallas kernels for 0%

profile of v3, /device:TPU:1, one launch (start us, length us, event | category | flops | bytes accessed | tf_op | source)
XLA Modules:
  0.0 93.2 jit_solution(17876347900614307951)
XLA Ops:
  0.6 0.7 pad_add_fusion.own
  1.4 10.2 %collective-permute-start = (s32[3,2,8,128]{3,2,1,0:T(8,128)S(1)}, s32[3,2,8,128]{3,2,1,0:T(8,128)S(1)}, u32[]{:S(2)}, u32[]{:S(2)}) collective-permute-start(s32[3,2,8,128]{3,2,1,0:T(8,128)S(1)} %pad_add_fusion.own), channel_id=1, source_target_pairs={{16,32},{48,64},{80,96},{112,128},{144,160},{176,192},{208,224},{2... | collective-permute-start | bytes 73736 | tf_op jit(solution)/shard_map/ppermute | solution.py:229
  11.6 1.8 %all-gather = s32[6,2,8,128]{3,2,1,0:T(8,128)S(1)} all-gather(s32[3,2,8,128]{3,2,1,0:T(8,128)S(1)} %pad_add_fusion.own), channel_id=2, replica_groups=mesh['y'=4,'zh'=4,'c'=2,'x'=4,'zl'=4] {'c'}, dimensions={0}, use_global_device_ids=true | all-gather | bytes 73728 | tf_op jit(solution)/shard_map/all_gather | solution.py:249
  13.4 0.0 collective-permute-done.across
  13.5 0.8 broadcast_select_fusion
  14.3 3.5 %collective-permute-start.1 = (s32[3,4,2,128]{3,2,1,0:T(2,128)S(1)}, s32[3,4,2,128]{3,2,1,0:T(2,128)S(1)}, u32[]{:S(2)}, u32[]{:S(2)}) collective-permute-start(s32[3,4,2,128]{3,2,1,0:T(2,128)S(1)} %bitcast.23), channel_id=1, source_target_pairs={{0,1},{2,3},{4,5},{6,7},{8,9},{10,11},{12,13},{14,15},{1,0},{3,2},... | collective-permute-start | bytes 36872 | tf_op jit(solution)/shard_map/ppermute | solution.py:229
  17.8 0.7 collective-permute-start.2
  18.5 0.8 broadcast_in_dim.6
  19.3 0.1 reshape.19
  19.3 0.1 copy.10.cen
  19.5 0.1 stack.31.info
  19.5 0.0 collective-permute-done.1.even
  19.5 0.0 collective-permute-done.2.odd
  19.5 6.5 %fields.1 = (f32[192,2048]{1,0:T(8,128)S(1)}, f32[192,128]{1,0:T(8,128)S(1)}) custom-call(s32[6]{0:T(128)S(1)} %stack.31.info, s32[3,2,8,128]{3,2,1,0:T(8,128)S(1)} %pad_add_fusion.own, s32[2,3,2,8,128]{4,3,2,1,0:T(8,128)S(1)} %bitcast.14, s32[3,2,8,128]{3,2,1,0:T(8,128)S(1)} %collective-permute-done.across, ...), custom_call_target="tpu_custom_call" | custom-call | tf_op jit(solution)/shard_map/fields/pallas_call | solution.py:263
  26.1 23.9 %all_to_all.19 = f32[32,6,128]{2,1,0:T(8,128)S(1)} all-to-all(f32[32,6,128]{2,1,0:T(8,128)S(1)} %all_to_all.12), channel_id=1, replica_groups=mesh['y'=4,'zh'=4,'c'=2,'x'=4,'zl'=4] {'y','c','x'}, dimensions={0} | all-to-all | bytes 196608 | tf_op jit(solution)/shard_map/all_to_all | solution.py:235
  50.0 21.8 %all_to_all.20 = f32[16,6,128]{2,1,0:T(8,128)S(1)} all-to-all(f32[16,6,128]{2,1,0:T(8,128)S(1)} %broadcast_in_dim.7), channel_id=1, replica_groups=mesh['y'=4,'zh'=4,'c'=2,'x'=4,'zl'=4] {'zh','zl'}, dimensions={0} | all-to-all | bytes 98304 | tf_op jit(solution)/shard_map/all_to_all | solution.py:236
  71.9 12.9 %all_to_all.21 = f32[32,6,128]{2,1,0:T(8,128)S(1)} all-to-all(f32[32,6,128]{2,1,0:T(8,128)S(1)} %broadcast_in_dim.8), channel_id=1, replica_groups=mesh['y'=4,'zh'=4,'c'=2,'x'=4,'zl'=4] {'y','c','x'}, dimensions={0} | all-to-all | bytes 196608 | tf_op jit(solution)/shard_map/all_to_all | solution.py:237
  84.8 8.4 %solve.1 = (f32[1536,128]{1,0:T(8,128)}, f32[96,96]{1,0:T(8,128)}) custom-call(f32[192,128]{1,0:T(8,128)S(1)} %reshape.20.pay, f32[192,2048]{1,0:T(8,128)S(1)} %get-tuple-element.7.lh), custom_call_target="tpu_custom_call" | custom-call | tf_op jit(solution)/shard_map/solve/pallas_call | solution.py:284
  (9 shorter events, 0.1 us)
Async XLA Ops:
  1.4 12.1 %collective-permute-start = (s32[3,2,8,128]{3,2,1,0:T(8,128)S(1)}, s32[3,2,8,128]{3,2,1,0:T(8,128)S(1)}, u32[]{:S(2)}, u32[]{:S(2)}) collective-permute-start(s32[3,2,8,128]{3,2,1,0:T(8,128)S(1)} %pad_add_fusion.own), channel_id=1, source_target_pairs={{16,32},{48,64},{80,96},{112,128},{144,160},{176,192},{208,224},{2... | collective-permute-start | bytes 73736 | tf_op jit(solution)/shard_map/ppermute | solution.py:229
  14.3 5.3 %collective-permute-start.1 = (s32[3,4,2,128]{3,2,1,0:T(2,128)S(1)}, s32[3,4,2,128]{3,2,1,0:T(2,128)S(1)}, u32[]{:S(2)}, u32[]{:S(2)}) collective-permute-start(s32[3,4,2,128]{3,2,1,0:T(2,128)S(1)} %bitcast.23), channel_id=1, source_target_pairs={{0,1},{2,3},{4,5},{6,7},{8,9},{10,11},{12,13},{14,15},{1,0},{3,2},... | collective-permute-start | bytes 36872 | tf_op jit(solution)/shard_map/ppermute | solution.py:229
  17.8 1.7 %collective-permute-start.2 = (s32[3,4,2,128]{3,2,1,0:T(2,128)S(1)}, s32[3,4,2,128]{3,2,1,0:T(2,128)S(1)}, u32[]{:S(2)}, u32[]{:S(2)}) collective-permute-start(s32[3,4,2,128]{3,2,1,0:T(2,128)S(1)} %get-tuple-element.10), channel_id=1, source_target_pairs={{1,2},{3,4},{5,6},{7,8},{9,10},{11,12},{13,14},{2,1},{4,3},{6,5},{... | collective-permute-start | bytes 36872 | tf_op jit(solution)/shard_map/ppermute | solution.py:229

commit v4 on v3

v4 whole, which is shorter than its diff:
```python
import functools

import jax
import jax.numpy as jnp
import numpy as np
from jax import lax
from jax.experimental import pallas as pl
from jax.experimental.pallas import tpu as pltpu
from jax.sharding import Mesh, PartitionSpec as P

BODIES = 16
MODES = 6
COLS = BODIES * MODES
FOLD = 4 * MODES
GX = ("y", "zh", "c")
GY = ("x", "zl")
NEAR = ("y", "c", "x")
FAR = ("zh", "zl")
F32 = jnp.float32


def dot(left, right, dims):
    return lax.dot_general(
        left, right, (dims, ((), ())), precision=lax.Precision.HIGHEST, preferred_element_type=F32
    )


def mm(left, right):
    return dot(left, right, ((1,), (0,)))


THIRD = COLS // 3


def upper(size):
    r = lax.broadcasted_iota(jnp.int32, (size, size), 0)
    return r <= lax.broadcasted_iota(jnp.int32, (size, size), 1)


def on_diagonal(size):
    r = lax.broadcasted_iota(jnp.int32, (size, size), 0)
    return r == lax.broadcasted_iota(jnp.int32, (size, size), 1)


def chosen(shape, offset):
    r = lax.broadcasted_iota(jnp.int32, shape, 0) - offset
    c = lax.broadcasted_iota(jnp.int32, shape, 1)
    inside = (r >= 0) & (r < FOLD)
    return ((r - c + 2 * COLS) % MODES == 0).astype(F32) * inside.astype(F32)


def shared(left, right):
    size = left.shape[0]
    shape = (size, size + 1)
    r = lax.broadcasted_iota(jnp.int32, shape, 0)
    low = lax.broadcasted_iota(jnp.int32, shape, 1) <= r
    blank = jnp.zeros((size, 1), F32)
    return jnp.where(low, jnp.concatenate([right, blank], axis=1), jnp.concatenate([blank, left], axis=1))


def unshared(both):
    size = both.shape[0]
    left, right = both[:, 1 : size + 1], both[:, 0:size]
    keep = upper(size)
    return jnp.where(keep, left, left.T), jnp.where(keep, right.T, right)


def unpacked(pay):
    t = THIRD
    first, second = unshared(pay[0:COLS, 0 : COLS + 1])
    at = COLS + 1
    r = lax.broadcasted_iota(jnp.int32, (COLS, COLS), 0)
    c = lax.broadcasted_iota(jnp.int32, (COLS, COLS), 1)
    zeroth = mm(pay[0:COLS, at : at + MODES], chosen((MODES, COLS), 0))
    zeroth = jnp.where(((r * 43) >> 8) == ((c * 43) >> 8), zeroth, 0.0)
    at, half = at + MODES, t // 2 + 1
    middle, end = unshared(
        jnp.concatenate([pay[0:t, at : at + half], pay[t : 2 * t, at : at + half - 1]], axis=1)
    )
    block = [pay[COLS : COLS + t, t * k : t * (k + 1)] for k in range(4)]
    third = jnp.concatenate(
        [
            jnp.concatenate([block[3], block[0], block[1]], axis=1),
            jnp.concatenate([block[0].T, middle, block[2]], axis=1),
            jnp.concatenate([block[1].T, block[2].T, end], axis=1),
        ],
        axis=0,
    )
    return zeroth, first, second, third


class Rows:
    def __init__(self, nx, ny, nz, base, cx, cy, fext, qext):
        self.nx, self.ny, self.nz, self.ey = nx, ny, nz, ny + 4
        self.base, self.cx, self.cy, self.fext, self.qext = base, cx, cy, fext, qext
        col = lax.broadcasted_iota(jnp.int32, (COLS, nz), 0)
        body = (col * 43) >> 8
        mode = col - MODES * body
        self.bodyf = body.astype(F32)
        self.one = [(mode == m).astype(F32) for m in range(MODES)]
        self.step3 = self.one[3] * (3.0 / nz)
        self.step4 = self.one[4] * (3.0 / nz)

    def describe(self, cells, layer, rows, shifts):
        nz, base = self.nz, self.base
        lane = lax.broadcasted_iota(jnp.int32, (1, nz), 1)
        tags, index, fluid = cells
        shifted = index + (index >= 13).astype(jnp.int32)
        part_x = (shifted >= 9).astype(jnp.int32) + (shifted >= 18).astype(jnp.int32)
        rest = shifted - 9 * part_x
        part_y = (rest >= 3).astype(jnp.int32) + (rest >= 6).astype(jnp.int32)
        part_z = rest - 3 * part_y
        comps = [(part - 1).astype(F32) for part in (part_x, part_y, part_z)]
        inverse = 1.0 / jnp.sqrt(comps[0] * comps[0] + comps[1] * comps[1] + comps[2] * comps[2])
        fl = fluid.astype(F32)
        values = [comp * inverse * fl for comp in comps] + [tags.astype(F32)]
        for m, value in enumerate(values):
            base[m, layer, rows] = value
            if shifts:
                after = pltpu.roll(value, nz - 1, value.ndim - 1)
                before = pltpu.roll(value, 1, value.ndim - 1)
                if m == 3:
                    after = jnp.where(lane == nz - 1, -1.0, after)
                    before = jnp.where(lane == 0, -1.0, before)
                base[4 + m, layer, rows] = after
                base[8 + m, layer, rows] = before
        base[12, layer, rows] = fl

    def coefficients(self, info, cen):
        nz, one = self.nz, self.one
        start_x, start_y, count_x, count_y = (info[k] for k in range(4))
        column = lax.broadcasted_iota(jnp.int32, (COLS, BODIES), 0)
        mine = ((column * 43) >> 8) == lax.broadcasted_iota(jnp.int32, (COLS, BODIES), 1)
        spread = dot(mine.astype(F32), cen[...], ((1,), (1,)))
        cen_x, cen_y, cen_z = (jnp.broadcast_to(spread[:, d : d + 1], (COLS, nz)) for d in range(3))
        lane = lax.broadcasted_iota(jnp.int32, (COLS, nz), 1)
        lever_z = 3.0 * ((lane.astype(F32) + 0.5) * (1.0 / nz) - cen_z)
        coef_x0 = one[0] + one[4] * lever_z
        coef_y0 = one[1] - one[3] * lever_z
        for i in range(self.nx + 4):
            lever = 3.0 * (((start_x + (i - 2)).astype(F32) + 0.5) / count_x.astype(F32) - cen_x)
            self.cx[0, i] = coef_y0 + one[5] * lever
            self.cx[1, i] = -one[4] * lever
        for j in range(self.ey):
            y = j if j < self.ny + 2 else j - self.ey
            lever = 3.0 * (((start_y + y).astype(F32) + 0.5) / count_y.astype(F32) - cen_y)
            self.cy[0, j] = coef_x0 - one[5] * lever
            self.cy[1, j] = one[2] + one[3] * lever

    def at(self, j):
        return jnp.where(j < 0, j + self.ey, jnp.where(j >= self.ey, j - self.ey, j))

    def row(self, which, i, j):
        return jnp.broadcast_to(self.base[which, i, pl.ds(j, 1), :], (COLS, self.nz))

    def sample(self, first, i, j, coefs):
        value = self.row(first, i, j) * coefs[0]
        value = value + self.row(first + 1, i, j) * coefs[1] + self.row(first + 2, i, j) * coefs[2]
        return jnp.where(self.row(first + 3, i, j) == self.bodyf, value, 0.0)

    def coefs(self, i, j):
        return self.cy[0, j], self.cx[0, i], self.cy[1, j] + self.cx[1, i]

    def forcing(self, i, j):
        j = self.at(j)
        self.fext[i, j] = self.sample(0, i, j, self.coefs(i, j))

    def both(self, i, j):
        j = self.at(j)
        x, y, z = self.coefs(i, j)
        self.fext[i, j] = self.sample(0, i, j, (x, y, z))
        after = self.sample(4, i, j, (x + self.step4, y - self.step3, z))
        self.qext[i, j] = after + self.sample(8, i, j, (x - self.step4, y + self.step3, z))

    def apply(self, src, i, j, field, along_z):
        beside = src[i + 1, j] + src[i - 1, j]
        beside = beside + src[i, self.at(j + 1)] + src[i, self.at(j - 1)]
        beside = beside + along_z
        return field + self.row(12, i, j) * (5.0 * field - beside)

    def operated(self, i, j):
        j = self.at(j)
        self.qext[i, j] = self.apply(self.fext, i, j, self.fext[i, j], self.qext[i, j])

    def collect(self, i, j, cells, lh, rh):
        nz = self.nz
        lane = lax.broadcasted_iota(jnp.int32, (COLS, nz), 1)
        forcing, field = self.fext[i, j], self.qext[i, j]
        up = jnp.where(lane >= 1, pltpu.roll(field, 1, 1), 0.0)
        down = jnp.where(lane < nz - 1, pltpu.roll(field, nz - 1, 1), 0.0)
        lh[0:COLS, cells] = forcing
        lh[COLS : 2 * COLS, cells] = field
        rh[0:COLS, cells] = field
        rh[COLS : 2 * COLS, cells] = self.apply(self.qext, i, j, field, up + down)
        fold = forcing[0:FOLD]
        for k in range(1, COLS // FOLD):
            fold = fold + forcing[k * FOLD : (k + 1) * FOLD]
        rh[2 * COLS : 2 * COLS + FOLD, cells] = fold


    @staticmethod
    def pack(grams, pay):
        first, second = grams[0:COLS, 0:COLS], grams[COLS : 2 * COLS, 0:COLS]
        third = grams[COLS : 2 * COLS, COLS : 2 * COLS]
        t = THIRD
        zeroth = mm(grams[0:COLS, 2 * COLS : 2 * COLS + FOLD], chosen((FOLD, MODES), 0))
        blocks = [[third[t * p : t * (p + 1), t * q : t * (q + 1)] for q in range(3)] for p in range(3)]
        ends = shared(blocks[1][1], blocks[2][2])
        half = t // 2 + 1
        ends = jnp.concatenate([ends[:, :half], jnp.pad(ends[:, half:], ((0, t), (0, 1)))], axis=0)
        unused = jnp.zeros((COLS, 128 - COLS - 1 - MODES - half), F32)
        pay[0:COLS, :] = jnp.concatenate([shared(first, second), zeroth, ends, unused], axis=1)
        pay[COLS : COLS + t, :] = jnp.concatenate([blocks[0][1], blocks[0][2], blocks[1][2], blocks[0][0]], axis=1)


def own_kernel(nx, ny, nz, info, own, cen_hbm, base, cx, cy, fext, qext, cen, sem):
    centers = pltpu.make_async_copy(cen_hbm, cen, sem)
    centers.start()
    rows = Rows(nx, ny, nz, base, cx, cy, fext, qext)
    for layer in range(nx):
        rows.describe([own[k, layer] for k in range(3)], layer + 2, pl.ds(0, ny), True)
    centers.wait()
    rows.coefficients(info, cen)
    for i in range(2, nx + 2):

        @pl.loop(0, ny, unroll=True)
        def _(j, i=i):
            rows.both(i, j)


def inner_kernel(nx, ny, nz, info, across, pair, cx, cy, base_in, fext_in, qext_in, base, fext, qext, lh, gram, rh):
    del base_in, fext_in, qext_in
    rows = Rows(nx, ny, nz, base, cx, cy, fext, qext)
    core = info[4]
    other, beyond = pair[...], across[...]
    before = jnp.where(core == 0, beyond, other)
    after = jnp.where(core == 0, other, beyond)
    for layer in range(nx):
        rows.describe([before[k, layer] for k in range(3)], layer, pl.ds(0, ny), layer == nx - 1)
        rows.describe([after[k, layer] for k in range(3)], layer + 2 + nx, pl.ds(0, ny), layer == 0)
    for i in (0, 1, nx + 2, nx + 3):

        @pl.loop(0, ny, unroll=True)
        def _(j, i=i):
            if i in (1, nx + 2):
                rows.both(i, j)
            else:
                rows.forcing(i, j)

    for i in range(1, nx + 3):

        @pl.loop(1, ny - 1, unroll=True)
        def _(j, i=i):
            rows.operated(i, j)

    for i in range(2, nx + 2):

        @pl.loop(0, ny - 4, unroll=True)
        def _(k, i=i):
            cells = pl.ds(pl.multiple_of(((i - 2) * (ny - 4) + k) * nz, nz), nz)
            rows.collect(i, k + 2, cells, lh, rh)

    gram[...] = dot(lh[...], rh[...], ((1,), (1,)))


def outer_kernel(
    nx, ny, nz, info, odd, even, cx, cy, base_in, fext_in, qext_in, gram, base, fext, qext, lh, pay, rh
):
    del base_in, fext_in, qext_in
    rows = Rows(nx, ny, nz, base, cx, cy, fext, qext)
    parity = info[5]
    above = jnp.where(parity == 0, even[...], odd[...])
    below = jnp.where(parity == 0, odd[...], even[...])
    for layer in range(nx + 2):
        rows.describe([above[k, layer] for k in range(3)], layer + 1, pl.ds(ny, 2), True)
        rows.describe([below[k, layer] for k in range(3)], layer + 1, pl.ds(ny + 2, 2), True)
    for i in range(1, nx + 3):
        reach = 2 if 2 <= i < nx + 2 else 1
        for j in list(range(-reach, 0)) + list(range(ny, ny + reach)):
            if j in (-1, ny) and 2 <= i < nx + 2:
                rows.both(i, j)
            else:
                rows.forcing(i, j)
    for i in range(1, nx + 3):
        inside = 2 <= i < nx + 2

        @pl.loop(0, 2, unroll=True)
        def _(k, i=i):
            rows.operated(i, k * (ny - 1))

        if inside:

            @pl.loop(0, 2, unroll=True)
            def _(k, i=i):
                rows.operated(i, k * (ny + 1) - 1)

    for i in range(2, nx + 2):

        @pl.loop(0, 4, unroll=True)
        def _(k, i=i):
            cells = pl.ds(pl.multiple_of(((i - 2) * 4 + k) * nz, nz), nz)
            rows.collect(i, jnp.where(k < 2, k, k + ny - 4), cells, lh, rh)

    rows.pack(gram[...] + dot(lh[...], rh[...], ((1,), (1,))), pay)


def inverse_spd(matrix, work):
    size = matrix.shape[0]
    r = lax.broadcasted_iota(jnp.int32, (size, size), 0)
    c = lax.broadcasted_iota(jnp.int32, (size, size), 1)
    diagonal = jnp.where(r == c, matrix, 0.0)
    scale_r = lax.rsqrt(jnp.sum(diagonal, axis=1, keepdims=True))
    scale_c = lax.rsqrt(jnp.sum(diagonal, axis=0, keepdims=True))
    scaled = matrix * scale_r * scale_c
    square = mm(scaled, scaled)
    bound = jnp.max(jnp.sum(jnp.abs(square), axis=0, keepdims=True), axis=1, keepdims=True)
    weight = jnp.minimum(1.0, 1.9 * lax.rsqrt(bound))
    eye = (r == c).astype(F32)
    twice = 2.0 * eye - weight * scaled
    work[0:size] = twice
    work[size : 2 * size] = twice - eye - weight * (scaled - weight * square)

    def longer(carry):
        power = work[size : 2 * size]
        more = mm(work[...], power)
        work[0:size] = work[0:size] + more[:size]
        work[size : 2 * size] = more[size:]
        return carry[0] + 1, jnp.sum(power * power) > 3e-7

    lax.while_loop(lambda carry: (carry[0] < 28) & carry[1], longer, (jnp.int32(0), jnp.bool_(True)))
    return work[0:size] * (weight * scale_r) * scale_c


def solve_kernel(nx, ny, nz, scale, pay, inner, outer, out, added, work):
    zeroth, first, second, third = unpacked(pay)
    center = jnp.where(on_diagonal(COLS), second / first, 0.0)
    shift = jnp.sum(jnp.sum(center, axis=1, keepdims=True), axis=0, keepdims=True) * (1.0 / COLS)
    cross = second - shift * first
    energy = jnp.concatenate(
        [
            jnp.concatenate([first, cross], axis=1),
            jnp.concatenate([cross, third - shift * (second + cross)], axis=1),
        ],
        axis=0,
    )
    solved = mm(inverse_spd(energy, work), jnp.concatenate([zeroth, first - shift * zeroth], axis=0))
    later = solved[COLS:]
    early = solved[:COLS] - shift * later
    coeffs = jnp.concatenate([early, later], axis=0)
    rows = nx * ny
    for lh, places in ((inner, range(2, ny - 2)), (outer, [0, 1, ny - 2, ny - 1])):
        values = dot(coeffs, lh[...], ((0,), (0,)))
        for k, (i, j) in enumerate((i, j) for i in range(nx) for j in places):
            out[pl.ds(i * ny + j, COLS, stride=rows), :] = values[:, k * nz : (k + 1) * nz]
    added[...] = (mm(zeroth, early) + mm(first, later)) * scale


def swap(array, axes, start):
    size = lax.axis_size(axes)
    pairs = [(i, i + 1) for i in range(start, size - 1, 2)]
    return lax.ppermute(array, axes, pairs + [(j, i) for i, j in pairs])


def reduced(part):
    near, far = (lax.axis_size(axes) for axes in (NEAR, FAR))
    rows, lanes = part.shape
    piece = lax.all_to_all(part, NEAR, 0, 0, tiled=True).reshape(near, rows // near, lanes).sum(0)
    piece = lax.all_to_all(jnp.broadcast_to(piece[None], (far,) + piece.shape), FAR, 0, 0, tiled=True).sum(0)
    return lax.all_to_all(
        jnp.broadcast_to(piece[None], (near,) + piece.shape), NEAR, 0, 0, tiled=True
    ).reshape(rows, lanes)


def shards(surface_tags, normal_index, fluid_mask, body_centers):
    nx, ny, nz = surface_tags.shape
    count_x = nx * lax.axis_size(GX)
    count_y = ny * lax.axis_size(GY)
    at_x, at_y, core = lax.axis_index(GX), lax.axis_index(GY), lax.axis_index("c")
    own = lax.optimization_barrier(jnp.stack([surface_tags, normal_index, fluid_mask]))
    across = swap(own, GX, 1)
    pair = lax.ppermute(own, "c", [(0, 1), (1, 0)])
    before = jnp.where(core == 1, pair, across)[:, nx - 1 :]
    after = jnp.where(core == 0, pair, across)[:, :1]
    near = jnp.concatenate([before, own, after], axis=1)
    first, last = near[:, :, :2], near[:, :, ny - 2 :]
    parity = at_y % 2
    even = swap(jnp.where(parity == 0, last, first), GY, 0)
    odd = swap(jnp.where(parity == 0, first, last), GY, 1)
    info = jnp.stack(
        [at_x * nx, at_y * ny, jnp.int32(count_x), jnp.int32(count_y), core, parity]
    ).astype(jnp.int32)
    half = nx * ny * nz // 2
    ex, ey = nx + 4, ny + 4
    vmem = pl.BlockSpec(memory_space=pltpu.VMEM)
    smem = pl.BlockSpec(memory_space=pltpu.SMEM)

    def shape(*dims):
        return jax.ShapeDtypeStruct(dims, F32)

    def call(kernel, outs, ins, scratch, flops, aliases, name, last=vmem):
        return pl.pallas_call(
            functools.partial(kernel, nx, ny, nz),
            out_shape=outs,
            in_specs=[smem] + [vmem] * (len(ins) - 2) + [last],
            out_specs=tuple(vmem for _ in outs),
            scratch_shapes=scratch,
            input_output_aliases=aliases,
            compiler_params=pltpu.CompilerParams(vmem_limit_bytes=24 * 1024 * 1024),
            cost_estimate=pl.CostEstimate(flops=flops, bytes_accessed=8 * 1024 * 1024, transcendentals=0),
            name=name,
        )(*ins)

    base, field = shape(13, ex, ey, nz), shape(ex, ey, COLS, nz)
    base, cx, cy, fext, qext = call(
        own_kernel, (base, shape(2, ex, COLS, nz), shape(2, ey, COLS, nz), field, field),
        (info, own, body_centers.T), [pltpu.VMEM((3, BODIES), F32), pltpu.SemaphoreType.DMA], 1 << 28, {}, "own_rows",
        pl.BlockSpec(memory_space=pltpu.HBM),
    )
    rh = [pltpu.VMEM((2 * COLS + FOLD, half), F32)]
    base, fext, qext, inner, gram = call(
        inner_kernel,
        (shape(*base.shape), shape(*fext.shape), shape(*qext.shape), shape(2 * COLS, half), shape(2 * COLS, 2 * COLS + FOLD)),
        (info, across, pair, cx, cy, base, fext, qext), rh, 1 << 29, {5: 0, 6: 1, 7: 2}, "inner_rows",
    )
    _, _, _, outer, pay = call(
        outer_kernel,
        (shape(*base.shape), shape(*fext.shape), shape(*qext.shape), shape(2 * COLS, half), shape(COLS + THIRD, 128)),
        (info, odd, even, cx, cy, base, fext, qext, gram), rh, 1 << 29, {5: 0, 6: 1, 7: 2}, "outer_rows",
    )
    pay = reduced(pay)
    scale = 8.0 * BODIES / (count_x * count_y * nz)
    pressure, added = pl.pallas_call(
        functools.partial(solve_kernel, nx, ny, nz, scale),
        out_shape=(
            jax.ShapeDtypeStruct((COLS * nx * ny, nz), F32),
            jax.ShapeDtypeStruct((COLS, COLS), F32),
        ),
        in_specs=[vmem] * 3,
        out_specs=(vmem, vmem),
        scratch_shapes=[pltpu.VMEM((4 * COLS, 2 * COLS), F32)],
        compiler_params=pltpu.CompilerParams(vmem_limit_bytes=24 * 1024 * 1024),
        name="solve",
    )(pay, inner, outer)
    return pressure.reshape(COLS, nx, ny, nz), added


def solution(mesh):
    split = Mesh(np.asarray(mesh.devices).reshape(4, 4, 2, 4, 4), GX + GY)
    return jax.shard_map(
        shards,
        mesh=split,
        in_specs=(P(GX, GY, None), P(GX, GY, None), P(GX, GY, None), P()),
        out_specs=(P(None, GX, GY, None), P()),
        check_vma=False,
    )
```

time: 93.8 us -> 83.3 us (0.89)
  blocking collectives: 60.5 us -> 47.8 us
  starting transfers between devices: 14.4 us -> 19.2 us
  Pallas kernels: 14.9 us -> 13.4 us
    all_to_all x1, blocking collectives: 23.9 us -> 16.8 us  [reduced(): lax.all_to_all(part, NEAR, 0, 0, tiled=True)]
    all_to_all x1, blocking collectives: 21.8 us -> 18.7 us  [reduced(): lax.all_to_all(jnp.broadcast_to(piece[None], (far,) + piece.shape), FAR,...]
    ppermute x3, starting transfers between devices: 14.4 us -> 17.3 us  [swap(): return lax.ppermute(array, axes, pairs + [(j, i) for i, j in pairs])]
    ppermute x0 -> x1, starting transfers between devices: none -> 1.92 us  [shards(): pair = lax.ppermute(own, 'c', [(0, 1), (1, 0)])]
    all_gather x1 -> x0, blocking collectives: 1.84 us -> none  [shards(): pair = lax.all_gather(own, 'c')]
    pallas_call x2 -> x4, Pallas kernels: 14.9 us -> 13.4 us  [the longest x3 7.53 us: call(): pl.pallas_call(functools.partial(kernel, nx, ny, nz), out_shape=outs, in_...]
  transfers between devices with their start and end apart: 3 -> 4, of which waited for: 0 -> 0; matrix products, arithmetic and copies ran while one was open for 1% -> 0% of each run, Pallas kernels for 0% -> 6%
where the time goes in v4:
time: 83.3 us; the launch traced here: 82.9 us
  blocking collectives  47.8 us (57%)
  starting transfers between devices  19.2 us (23%)
  Pallas kernels  13.4 us (16%)
    all_to_all x1, blocking collectives, reduced(): lax.all_to_all(jnp.broadcast_to(piece[None], (far,) + piece.shape), FAR,...  18.7 us
    ppermute x3, starting transfers between devices, swap(): return lax.ppermute(array, axes, pairs + [(j, i) for i, j in pairs])  17.3 us
    all_to_all x1, blocking collectives, reduced(): lax.all_to_all(part, NEAR, 0, 0, tiled=True)  16.8 us
    all_to_all x1, blocking collectives, reduced(): lax.all_to_all(jnp.broadcast_to(piece[None], (near,) + piece.shape), NEAR...  12.4 us
    pallas_call x3, Pallas kernels, call(): pl.pallas_call(functools.partial(kernel, nx, ny, nz), out_shape=outs, in_...  7.53 us
    pallas_call x1, Pallas kernels, shards(): pl.pallas_call(functools.partial(solve_kernel, nx, ny, nz, scale), out_sh...  5.87 us
    ppermute x1, starting transfers between devices, shards(): pair = lax.ppermute(own, 'c', [(0, 1), (1, 0)])  1.92 us
  transfers between devices with their start and end apart: 4, of which 0 were waited for; matrix products, arithmetic and copies ran while one was open for 0% of the time, Pallas kernels for 6%

profile of v4, /device:TPU:1, one launch (start us, length us, event | category | flops | bytes accessed | tf_op | source)
XLA Modules:
  0.0 82.9 jit_solution(11127513260448442711)
XLA Ops:
  0.6 0.7 pad_add_fusion.own
  1.4 10.2 %collective-permute-start.1 = (s32[3,2,8,128]{3,2,1,0:T(8,128)S(1)}, s32[3,2,8,128]{3,2,1,0:T(8,128)S(1)}, u32[]{:S(2)}, u32[]{:S(2)}) collective-permute-start(s32[3,2,8,128]{3,2,1,0:T(8,128)S(1)} %pad_add_fusion.own), channel_id=1, source_target_pairs={{16,32},{48,64},{80,96},{112,128},{144,160},{176,192},{208,224},{2... | collective-permute-start | bytes 73736 | tf_op jit(solution)/shard_map/ppermute | solution.py:361
  11.6 1.9 %collective-permute-start = (s32[3,2,8,128]{3,2,1,0:T(8,128)S(1)}, s32[3,2,8,128]{3,2,1,0:T(8,128)S(1)}, u32[]{:S(2)}, u32[]{:S(2)}) collective-permute-start(s32[3,2,8,128]{3,2,1,0:T(8,128)S(1)} %pad_add_fusion.own), channel_id=1, source_target_pairs={{0,16},{16,0},{1,17},{17,1},{2,18},{18,2},{3,19},{19,3},{4,20},{20... | collective-permute-start | bytes 73736 | tf_op jit(solution)/shard_map/ppermute | solution.py:381
  13.5 0.1 stack.31.info
  13.6 0.0 copy-start
  13.6 0.7 copy-done
  14.3 1.8 %own_rows.1 = (f32[13,6,12,128]{3,2,1,0:T(8,128)S(1)}, f32[2,6,96,128]{3,2,1,0:T(8,128)S(1)}, f32[2,12,96,128]{3,2,1,0:T(8,128)S(1)}, f32[6,12,96,128]{3,2,1,0:T(8,128)S(1)}, f32[6,12,96,128]{3,2,1,0:T(8,128)S(1)}) custom-call(s32[6]{0:T(128)S(1)} %stack.31.info, s32[3,2,8,128]{3,2,1,0:T(8,128)S(1)} %pad_add_fusion.own, f32[3,16]{1,0:T(4,128)S(1)} %bitcast.16), custom_call_target="tpu_custom_call" | custom-call | flops 268435456 | bytes 8388608 | tf_op jit(solution)/shard_map/own_rows/pallas_call | solution.py:401
  16.1 0.0 collective-permute-done.1.across
  16.1 0.0 collective-permute-done.pair
  16.2 0.7 collective-permute-start.2
  16.9 6.4 %collective-permute-start.3 = (s32[3,4,2,128]{3,2,1,0:T(2,128)S(1)}, s32[3,4,2,128]{3,2,1,0:T(2,128)S(1)}, u32[]{:S(2)}, u32[]{:S(2)}) collective-permute-start(s32[3,4,2,128]{3,2,1,0:T(2,128)S(1)} %get-tuple-element.30), channel_id=1, source_target_pairs={{0,1},{2,3},{4,5},{6,7},{8,9},{10,11},{12,13},{14,15},{1,0},{3,2},... | collective-permute-start | bytes 36872 | tf_op jit(solution)/shard_map/ppermute | solution.py:361
  23.3 3.2 %inner_rows.1 = (f32[13,6,12,128]{3,2,1,0:T(8,128)S(1)}, f32[6,12,96,128]{3,2,1,0:T(8,128)S(1)}, f32[6,12,96,128]{3,2,1,0:T(8,128)S(1)}, f32[192,1024]{1,0:T(8,128)S(1)}, f32[192,216]{1,0:T(8,128)S(1)}) custom-call(s32[6]{0:T(128)S(1)} %stack.31.info, ...), custom_call_target="tpu_custom_call", output_to_operand_aliasing={{0}: (5, {}), {1}: (6, {}), {2}: (7, {})} | custom-call | flops 536870912 | bytes 8388608 | tf_op jit(solution)/shard_map/inner_rows/pallas_call | solution.py:401
  26.5 0.0 collective-permute-done.2.odd
  26.5 0.0 collective-permute-done.3.even
  26.5 2.5 %outer_rows.1 = (f32[13,6,12,128]{3,2,1,0:T(8,128)S(1)}, f32[6,12,96,128]{3,2,1,0:T(8,128)S(1)}, f32[6,12,96,128]{3,2,1,0:T(8,128)S(1)}, f32[192,1024]{1,0:T(8,128)S(1)}, f32[128,128]{1,0:T(8,128)S(1)}) custom-call(s32[6]{0:T(128)S(1)} %stack.31.info, ...), custom_call_target="tpu_custom_call", output_to_operand_aliasing={{0}: (5, {}), {1}: (6, {}), {2}: (7, {})} | custom-call | flops 536870912 | bytes 8388608 | tf_op jit(solution)/shard_map/outer_rows/pallas_call | solution.py:401
  29.0 16.8 %all_to_all.19 = f32[32,4,128]{2,1,0:T(4,128)S(1)} all-to-all(f32[32,4,128]{2,1,0:T(4,128)S(1)} %bitcast.15), channel_id=1, replica_groups=mesh['y'=4,'zh'=4,'c'=2,'x'=4,'zl'=4] {'y','c','x'}, dimensions={0} | all-to-all | bytes 131072 | tf_op jit(solution)/shard_map/all_to_all | solution.py:367
  45.9 18.7 %all_to_all.20 = f32[16,4,128]{2,1,0:T(4,128)S(1)} all-to-all(f32[16,4,128]{2,1,0:T(4,128)S(1)} %broadcast_in_dim.4), channel_id=1, replica_groups=mesh['y'=4,'zh'=4,'c'=2,'x'=4,'zl'=4] {'zh','zl'}, dimensions={0} | all-to-all | bytes 65536 | tf_op jit(solution)/shard_map/all_to_all | solution.py:368
  64.6 12.4 %all_to_all.21 = f32[32,4,128]{2,1,0:T(4,128)S(1)} all-to-all(f32[32,4,128]{2,1,0:T(4,128)S(1)} %broadcast_in_dim.5), channel_id=1, replica_groups=mesh['y'=4,'zh'=4,'c'=2,'x'=4,'zl'=4] {'y','c','x'}, dimensions={0} | all-to-all | bytes 131072 | tf_op jit(solution)/shard_map/all_to_all | solution.py:369
  77.0 5.9 %solve.1 = (f32[1536,128]{1,0:T(8,128)}, f32[96,96]{1,0:T(8,128)}) custom-call(f32[128,128]{1,0:T(8,128)S(1)} %bitcast.14, f32[192,1024]{1,0:T(8,128)S(1)} %get-tuple-element.26.inner, f32[192,1024]{1,0:T(8,128)S(1)} %get-tuple-element.27.outer), custom_call_target="tpu_custom_call" | custom-call | tf_op jit(solution)/shard_map/solve/pallas_call | solution.py:432
  (7 shorter events, 0.1 us)
Async XLA Ops:
  1.4 14.8 %collective-permute-start.1 = (s32[3,2,8,128]{3,2,1,0:T(8,128)S(1)}, s32[3,2,8,128]{3,2,1,0:T(8,128)S(1)}, u32[]{:S(2)}, u32[]{:S(2)}) collective-permute-start(s32[3,2,8,128]{3,2,1,0:T(8,128)S(1)} %pad_add_fusion.own), channel_id=1, source_target_pairs={{16,32},{48,64},{80,96},{112,128},{144,160},{176,192},{208,224},{2... | collective-permute-start | bytes 73736 | tf_op jit(solution)/shard_map/ppermute | solution.py:361
  11.6 4.6 %collective-permute-start = (s32[3,2,8,128]{3,2,1,0:T(8,128)S(1)}, s32[3,2,8,128]{3,2,1,0:T(8,128)S(1)}, u32[]{:S(2)}, u32[]{:S(2)}) collective-permute-start(s32[3,2,8,128]{3,2,1,0:T(8,128)S(1)} %pad_add_fusion.own), channel_id=1, source_target_pairs={{0,16},{16,0},{1,17},{17,1},{2,18},{18,2},{3,19},{19,3},{4,20},{20... | collective-permute-start | bytes 73736 | tf_op jit(solution)/shard_map/ppermute | solution.py:381
  13.6 0.7 copy-start
  16.2 10.3 %collective-permute-start.2 = (s32[3,4,2,128]{3,2,1,0:T(2,128)S(1)}, s32[3,4,2,128]{3,2,1,0:T(2,128)S(1)}, u32[]{:S(2)}, u32[]{:S(2)}) collective-permute-start(s32[3,4,2,128]{3,2,1,0:T(2,128)S(1)} %bitcast.19), channel_id=1, source_target_pairs={{1,2},{3,4},{5,6},{7,8},{9,10},{11,12},{13,14},{2,1},{4,3},{6,5},{... | collective-permute-start | bytes 36872 | tf_op jit(solution)/shard_map/ppermute | solution.py:361
  16.9 9.6 %collective-permute-start.3 = (s32[3,4,2,128]{3,2,1,0:T(2,128)S(1)}, s32[3,4,2,128]{3,2,1,0:T(2,128)S(1)}, u32[]{:S(2)}, u32[]{:S(2)}) collective-permute-start(s32[3,4,2,128]{3,2,1,0:T(2,128)S(1)} %get-tuple-element.30), channel_id=1, source_target_pairs={{0,1},{2,3},{4,5},{6,7},{8,9},{10,11},{12,13},{14,15},{1,0},{3,2},... | collective-permute-start | bytes 36872 | tf_op jit(solution)/shard_map/ppermute | solution.py:361

commit v5 on v4

--- a/solution.py
+++ b/solution.py
@@ -314,18 +314,17 @@
     scaled = matrix * scale_r * scale_c
     square = mm(scaled, scaled)
     bound = jnp.max(jnp.sum(jnp.abs(square), axis=0, keepdims=True), axis=1, keepdims=True)
-    weight = jnp.minimum(1.0, 1.9 * lax.rsqrt(bound))
+    weight = lax.rsqrt(bound)
     eye = (r == c).astype(F32)
-    twice = 2.0 * eye - weight * scaled
-    work[0:size] = twice
-    work[size : 2 * size] = twice - eye - weight * (scaled - weight * square)
+    work[0:size] = (30.0 / 7.0) * eye - (25.0 / 7.0 * weight) * scaled
+    work[size : 2 * size] = eye - (30.0 / 7.0 * weight) * scaled + (25.0 / 7.0 * weight * weight) * square
 
     def longer(carry):
         power = work[size : 2 * size]
         more = mm(work[...], power)
         work[0:size] = work[0:size] + more[:size]
         work[size : 2 * size] = more[size:]
-        return carry[0] + 1, jnp.sum(power * power) > 3e-7
+        return carry[0] + 1, jnp.sum(power * power) > 2e-6
 
     lax.while_loop(lambda carry: (carry[0] < 28) & carry[1], longer, (jnp.int32(0), jnp.bool_(True)))
     return work[0:size] * (weight * scale_r) * scale_c

time: 83.3 us -> 82.8 us (level)
  no operation moved by 1% of the time
where the time goes in v5:
time: 82.8 us; the launch traced here: 82.4 us
  blocking collectives  47.8 us (58%)
  starting transfers between devices  19.2 us (23%)
  Pallas kernels  12.9 us (16%)
  other arithmetic  0.83 us (1%)
    all_to_all x1, blocking collectives, reduced(): lax.all_to_all(jnp.broadcast_to(piece[None], (far,) + piece.shape), FAR,...  18.7 us
    ppermute x3, starting transfers between devices, swap(): return lax.ppermute(array, axes, pairs + [(j, i) for i, j in pairs])  17.3 us
    all_to_all x1, blocking collectives, reduced(): lax.all_to_all(part, NEAR, 0, 0, tiled=True)  16.8 us
    all_to_all x1, blocking collectives, reduced(): lax.all_to_all(jnp.broadcast_to(piece[None], (near,) + piece.shape), NEAR...  12.4 us
    pallas_call x3, Pallas kernels, call(): pl.pallas_call(functools.partial(kernel, nx, ny, nz), out_shape=outs, in_...  7.53 us
    pallas_call x1, Pallas kernels, shards(): pl.pallas_call(functools.partial(solve_kernel, nx, ny, nz, scale), out_sh...  5.37 us
    ppermute x1, starting transfers between devices, shards(): pair = lax.ppermute(own, 'c', [(0, 1), (1, 0)])  1.92 us
  transfers between devices with their start and end apart: 4, of which 0 were waited for; matrix products, arithmetic and copies ran while one was open for 0% of the time, Pallas kernels for 6%

profile of v5, /device:TPU:1, one launch (start us, length us, event | category | flops | bytes accessed | tf_op | source)
XLA Modules:
  0.0 82.4 jit_solution(4813310718871378851)
XLA Ops:
  0.6 0.7 pad_add_fusion.own
  1.4 10.2 %collective-permute-start.1 = (s32[3,2,8,128]{3,2,1,0:T(8,128)S(1)}, s32[3,2,8,128]{3,2,1,0:T(8,128)S(1)}, u32[]{:S(2)}, u32[]{:S(2)}) collective-permute-start(s32[3,2,8,128]{3,2,1,0:T(8,128)S(1)} %pad_add_fusion.own), channel_id=1, source_target_pairs={{16,32},{48,64},{80,96},{112,128},{144,160},{176,192},{208,224},{2... | collective-permute-start | bytes 73736 | tf_op jit(solution)/shard_map/ppermute | solution.py:360
  11.6 1.9 %collective-permute-start = (s32[3,2,8,128]{3,2,1,0:T(8,128)S(1)}, s32[3,2,8,128]{3,2,1,0:T(8,128)S(1)}, u32[]{:S(2)}, u32[]{:S(2)}) collective-permute-start(s32[3,2,8,128]{3,2,1,0:T(8,128)S(1)} %pad_add_fusion.own), channel_id=1, source_target_pairs={{0,16},{16,0},{1,17},{17,1},{2,18},{18,2},{3,19},{19,3},{4,20},{20... | collective-permute-start | bytes 73736 | tf_op jit(solution)/shard_map/ppermute | solution.py:380
  13.5 0.1 stack.31.info
  13.6 0.0 copy-start
  13.6 0.7 copy-done
  14.3 1.8 %own_rows.1 = (f32[13,6,12,128]{3,2,1,0:T(8,128)S(1)}, f32[2,6,96,128]{3,2,1,0:T(8,128)S(1)}, f32[2,12,96,128]{3,2,1,0:T(8,128)S(1)}, f32[6,12,96,128]{3,2,1,0:T(8,128)S(1)}, f32[6,12,96,128]{3,2,1,0:T(8,128)S(1)}) custom-call(s32[6]{0:T(128)S(1)} %stack.31.info, s32[3,2,8,128]{3,2,1,0:T(8,128)S(1)} %pad_add_fusion.own, f32[3,16]{1,0:T(4,128)S(1)} %bitcast.16), custom_call_target="tpu_custom_call" | custom-call | flops 268435456 | bytes 8388608 | tf_op jit(solution)/shard_map/own_rows/pallas_call | solution.py:400
  16.1 0.0 collective-permute-done.1.across
  16.1 0.0 collective-permute-done.pair
  16.2 0.7 collective-permute-start.2
  16.9 6.4 %collective-permute-start.3 = (s32[3,4,2,128]{3,2,1,0:T(2,128)S(1)}, s32[3,4,2,128]{3,2,1,0:T(2,128)S(1)}, u32[]{:S(2)}, u32[]{:S(2)}) collective-permute-start(s32[3,4,2,128]{3,2,1,0:T(2,128)S(1)} %get-tuple-element.30), channel_id=1, source_target_pairs={{0,1},{2,3},{4,5},{6,7},{8,9},{10,11},{12,13},{14,15},{1,0},{3,2},... | collective-permute-start | bytes 36872 | tf_op jit(solution)/shard_map/ppermute | solution.py:360
  23.3 3.2 %inner_rows.1 = (f32[13,6,12,128]{3,2,1,0:T(8,128)S(1)}, f32[6,12,96,128]{3,2,1,0:T(8,128)S(1)}, f32[6,12,96,128]{3,2,1,0:T(8,128)S(1)}, f32[192,1024]{1,0:T(8,128)S(1)}, f32[192,216]{1,0:T(8,128)S(1)}) custom-call(s32[6]{0:T(128)S(1)} %stack.31.info, ...), custom_call_target="tpu_custom_call", output_to_operand_aliasing={{0}: (5, {}), {1}: (6, {}), {2}: (7, {})} | custom-call | flops 536870912 | bytes 8388608 | tf_op jit(solution)/shard_map/inner_rows/pallas_call | solution.py:400
  26.5 0.0 collective-permute-done.2.odd
  26.5 0.0 collective-permute-done.3.even
  26.5 2.5 %outer_rows.1 = (f32[13,6,12,128]{3,2,1,0:T(8,128)S(1)}, f32[6,12,96,128]{3,2,1,0:T(8,128)S(1)}, f32[6,12,96,128]{3,2,1,0:T(8,128)S(1)}, f32[192,1024]{1,0:T(8,128)S(1)}, f32[128,128]{1,0:T(8,128)S(1)}) custom-call(s32[6]{0:T(128)S(1)} %stack.31.info, ...), custom_call_target="tpu_custom_call", output_to_operand_aliasing={{0}: (5, {}), {1}: (6, {}), {2}: (7, {})} | custom-call | flops 536870912 | bytes 8388608 | tf_op jit(solution)/shard_map/outer_rows/pallas_call | solution.py:400
  29.0 16.8 %all_to_all.19 = f32[32,4,128]{2,1,0:T(4,128)S(1)} all-to-all(f32[32,4,128]{2,1,0:T(4,128)S(1)} %bitcast.15), channel_id=1, replica_groups=mesh['y'=4,'zh'=4,'c'=2,'x'=4,'zl'=4] {'y','c','x'}, dimensions={0} | all-to-all | bytes 131072 | tf_op jit(solution)/shard_map/all_to_all | solution.py:366
  45.9 18.7 %all_to_all.20 = f32[16,4,128]{2,1,0:T(4,128)S(1)} all-to-all(f32[16,4,128]{2,1,0:T(4,128)S(1)} %broadcast_in_dim.4), channel_id=1, replica_groups=mesh['y'=4,'zh'=4,'c'=2,'x'=4,'zl'=4] {'zh','zl'}, dimensions={0} | all-to-all | bytes 65536 | tf_op jit(solution)/shard_map/all_to_all | solution.py:367
  64.6 12.4 %all_to_all.21 = f32[32,4,128]{2,1,0:T(4,128)S(1)} all-to-all(f32[32,4,128]{2,1,0:T(4,128)S(1)} %broadcast_in_dim.5), channel_id=1, replica_groups=mesh['y'=4,'zh'=4,'c'=2,'x'=4,'zl'=4] {'y','c','x'}, dimensions={0} | all-to-all | bytes 131072 | tf_op jit(solution)/shard_map/all_to_all | solution.py:368
  77.0 5.4 %solve.1 = (f32[1536,128]{1,0:T(8,128)}, f32[96,96]{1,0:T(8,128)}) custom-call(f32[128,128]{1,0:T(8,128)S(1)} %bitcast.14, f32[192,1024]{1,0:T(8,128)S(1)} %get-tuple-element.26.inner, f32[192,1024]{1,0:T(8,128)S(1)} %get-tuple-element.27.outer), custom_call_target="tpu_custom_call" | custom-call | tf_op jit(solution)/shard_map/solve/pallas_call | solution.py:431
  (7 shorter events, 0.1 us)
Async XLA Ops:
  1.4 14.8 %collective-permute-start.1 = (s32[3,2,8,128]{3,2,1,0:T(8,128)S(1)}, s32[3,2,8,128]{3,2,1,0:T(8,128)S(1)}, u32[]{:S(2)}, u32[]{:S(2)}) collective-permute-start(s32[3,2,8,128]{3,2,1,0:T(8,128)S(1)} %pad_add_fusion.own), channel_id=1, source_target_pairs={{16,32},{48,64},{80,96},{112,128},{144,160},{176,192},{208,224},{2... | collective-permute-start | bytes 73736 | tf_op jit(solution)/shard_map/ppermute | solution.py:360
  11.6 4.6 %collective-permute-start = (s32[3,2,8,128]{3,2,1,0:T(8,128)S(1)}, s32[3,2,8,128]{3,2,1,0:T(8,128)S(1)}, u32[]{:S(2)}, u32[]{:S(2)}) collective-permute-start(s32[3,2,8,128]{3,2,1,0:T(8,128)S(1)} %pad_add_fusion.own), channel_id=1, source_target_pairs={{0,16},{16,0},{1,17},{17,1},{2,18},{18,2},{3,19},{19,3},{4,20},{20... | collective-permute-start | bytes 73736 | tf_op jit(solution)/shard_map/ppermute | solution.py:380
  13.6 0.7 copy-start
  16.2 10.3 %collective-permute-start.2 = (s32[3,4,2,128]{3,2,1,0:T(2,128)S(1)}, s32[3,4,2,128]{3,2,1,0:T(2,128)S(1)}, u32[]{:S(2)}, u32[]{:S(2)}) collective-permute-start(s32[3,4,2,128]{3,2,1,0:T(2,128)S(1)} %bitcast.19), channel_id=1, source_target_pairs={{1,2},{3,4},{5,6},{7,8},{9,10},{11,12},{13,14},{2,1},{4,3},{6,5},{... | collective-permute-start | bytes 36872 | tf_op jit(solution)/shard_map/ppermute | solution.py:360
  16.9 9.6 %collective-permute-start.3 = (s32[3,4,2,128]{3,2,1,0:T(2,128)S(1)}, s32[3,4,2,128]{3,2,1,0:T(2,128)S(1)}, u32[]{:S(2)}, u32[]{:S(2)}) collective-permute-start(s32[3,4,2,128]{3,2,1,0:T(2,128)S(1)} %get-tuple-element.30), channel_id=1, source_target_pairs={{0,1},{2,3},{4,5},{6,7},{8,9},{10,11},{12,13},{14,15},{1,0},{3,2},... | collective-permute-start | bytes 36872 | tf_op jit(solution)/shard_map/ppermute | solution.py:360

commit v6 on v5

--- a/solution.py
+++ b/solution.py
@@ -30,6 +30,9 @@
 
 
 THIRD = COLS // 3
+NEXT = MODES + 1
+PREVIOUS = 2 * NEXT
+MASK = 3 * NEXT
 
 
 def upper(size):
@@ -90,21 +93,21 @@
 
 
 class Rows:
-    def __init__(self, nx, ny, nz, base, cx, cy, fext, qext):
+    def __init__(self, nx, ny, nz, info, centers, base, fext, qext):
         self.nx, self.ny, self.nz, self.ey = nx, ny, nz, ny + 4
-        self.base, self.cx, self.cy, self.fext, self.qext = base, cx, cy, fext, qext
-        col = lax.broadcasted_iota(jnp.int32, (COLS, nz), 0)
-        body = (col * 43) >> 8
-        mode = col - MODES * body
-        self.bodyf = body.astype(F32)
-        self.one = [(mode == m).astype(F32) for m in range(MODES)]
-        self.step3 = self.one[3] * (3.0 / nz)
-        self.step4 = self.one[4] * (3.0 / nz)
-
-    def describe(self, cells, layer, rows, shifts):
-        nz, base = self.nz, self.base
-        lane = lax.broadcasted_iota(jnp.int32, (1, nz), 1)
+        self.info, self.centers = info, centers
+        self.base, self.fext, self.qext = base, fext, qext
+        row = lax.broadcasted_iota(jnp.int32, (FOLD, nz), 0)
+        body = (row * 43) >> 8
+        mode = row - MODES * body
+        self.is_mode = [mode == m for m in range(MODES)]
+        self.bodies = [(body + k * (FOLD // MODES)).astype(F32) for k in range(COLS // FOLD)]
+
+    def describe(self, cells, layer, rows, first_y, shifts):
+        nz, base, info = self.nz, self.base, self.info
         tags, index, fluid = cells
+        lane = lax.broadcasted_iota(jnp.int32, tags.shape, 1)
+        y = lax.broadcasted_iota(jnp.int32, tags.shape, 0) + (info[1] + first_y)
         shifted = index + (index >= 13).astype(jnp.int32)
         part_x = (shifted >= 9).astype(jnp.int32) + (shifted >= 18).astype(jnp.int32)
         rest = shifted - 9 * part_x
@@ -113,70 +116,55 @@
         comps = [(part - 1).astype(F32) for part in (part_x, part_y, part_z)]
         inverse = 1.0 / jnp.sqrt(comps[0] * comps[0] + comps[1] * comps[1] + comps[2] * comps[2])
         fl = fluid.astype(F32)
-        values = [comp * inverse * fl for comp in comps] + [tags.astype(F32)]
-        for m, value in enumerate(values):
+        n_x, n_y, n_z = (comp * inverse * fl for comp in comps)
+        place = [jnp.zeros(tags.shape, F32)] * 3
+        for b in range(BODIES):
+            here = tags == b
+            place = [jnp.where(here, self.centers[d, b], place[d]) for d in range(3)]
+        pos_x = ((info[0] + (layer - 2)).astype(F32) + 0.5) / info[2].astype(F32)
+        pos_y = (y.astype(F32) + 0.5) / info[3].astype(F32)
+        pos_z = (lane.astype(F32) + 0.5) * (1.0 / nz)
+        l_x, l_y, l_z = (3.0 * (pos - center) for pos, center in zip((pos_x, pos_y, pos_z), place))
+        values = [n_x, n_y, n_z, l_y * n_z - l_z * n_y, l_z * n_x - l_x * n_z, l_x * n_y - l_y * n_x]
+        for m, value in enumerate(values + [tags.astype(F32)]):
             base[m, layer, rows] = value
             if shifts:
-                after = pltpu.roll(value, nz - 1, value.ndim - 1)
-                before = pltpu.roll(value, 1, value.ndim - 1)
-                if m == 3:
+                after = pltpu.roll(value, nz - 1, 1)
+                before = pltpu.roll(value, 1, 1)
+                if m == MODES:
                     after = jnp.where(lane == nz - 1, -1.0, after)
                     before = jnp.where(lane == 0, -1.0, before)
-                base[4 + m, layer, rows] = after
-                base[8 + m, layer, rows] = before
-        base[12, layer, rows] = fl
-
-    def coefficients(self, info, cen):
-        nz, one = self.nz, self.one
-        start_x, start_y, count_x, count_y = (info[k] for k in range(4))
-        column = lax.broadcasted_iota(jnp.int32, (COLS, BODIES), 0)
-        mine = ((column * 43) >> 8) == lax.broadcasted_iota(jnp.int32, (COLS, BODIES), 1)
-        spread = dot(mine.astype(F32), cen[...], ((1,), (1,)))
-        cen_x, cen_y, cen_z = (jnp.broadcast_to(spread[:, d : d + 1], (COLS, nz)) for d in range(3))
-        lane = lax.broadcasted_iota(jnp.int32, (COLS, nz), 1)
-        lever_z = 3.0 * ((lane.astype(F32) + 0.5) * (1.0 / nz) - cen_z)
-        coef_x0 = one[0] + one[4] * lever_z
-        coef_y0 = one[1] - one[3] * lever_z
-        for i in range(self.nx + 4):
-            lever = 3.0 * (((start_x + (i - 2)).astype(F32) + 0.5) / count_x.astype(F32) - cen_x)
-            self.cx[0, i] = coef_y0 + one[5] * lever
-            self.cx[1, i] = -one[4] * lever
-        for j in range(self.ey):
-            y = j if j < self.ny + 2 else j - self.ey
-            lever = 3.0 * (((start_y + y).astype(F32) + 0.5) / count_y.astype(F32) - cen_y)
-            self.cy[0, j] = coef_x0 - one[5] * lever
-            self.cy[1, j] = one[2] + one[3] * lever
+                base[NEXT + m, layer, rows] = after
+                base[PREVIOUS + m, layer, rows] = before
+        base[MASK, layer, rows] = fl
 
     def at(self, j):
         return jnp.where(j < 0, j + self.ey, jnp.where(j >= self.ey, j - self.ey, j))
 
-    def row(self, which, i, j):
-        return jnp.broadcast_to(self.base[which, i, pl.ds(j, 1), :], (COLS, self.nz))
-
-    def sample(self, first, i, j, coefs):
-        value = self.row(first, i, j) * coefs[0]
-        value = value + self.row(first + 1, i, j) * coefs[1] + self.row(first + 2, i, j) * coefs[2]
-        return jnp.where(self.row(first + 3, i, j) == self.bodyf, value, 0.0)
-
-    def coefs(self, i, j):
-        return self.cy[0, j], self.cx[0, i], self.cy[1, j] + self.cx[1, i]
+    def row(self, which, i, j, rows):
+        return jnp.broadcast_to(self.base[which, i, pl.ds(j, 1), :], (rows, self.nz))
+
+    def sample(self, first, i, j):
+        value = self.row(first, i, j, FOLD)
+        for m in range(1, MODES):
+            value = jnp.where(self.is_mode[m], self.row(first + m, i, j, FOLD), value)
+        tag = self.row(first + MODES, i, j, FOLD)
+        return jnp.concatenate([jnp.where(tag == bodies, value, 0.0) for bodies in self.bodies], axis=0)
 
     def forcing(self, i, j):
         j = self.at(j)
-        self.fext[i, j] = self.sample(0, i, j, self.coefs(i, j))
+        self.fext[i, j] = self.sample(0, i, j)
 
     def both(self, i, j):
         j = self.at(j)
-        x, y, z = self.coefs(i, j)
-        self.fext[i, j] = self.sample(0, i, j, (x, y, z))
-        after = self.sample(4, i, j, (x + self.step4, y - self.step3, z))
-        self.qext[i, j] = after + self.sample(8, i, j, (x - self.step4, y + self.step3, z))
+        self.fext[i, j] = self.sample(0, i, j)
+        self.qext[i, j] = self.sample(NEXT, i, j) + self.sample(PREVIOUS, i, j)
 
     def apply(self, src, i, j, field, along_z):
         beside = src[i + 1, j] + src[i - 1, j]
         beside = beside + src[i, self.at(j + 1)] + src[i, self.at(j - 1)]
         beside = beside + along_z
-        return field + self.row(12, i, j) * (5.0 * field - beside)
+        return field + self.row(MASK, i, j, COLS) * (5.0 * field - beside)
 
     def operated(self, i, j):
         j = self.at(j)
@@ -213,14 +201,11 @@
         pay[COLS : COLS + t, :] = jnp.concatenate([blocks[0][1], blocks[0][2], blocks[1][2], blocks[0][0]], axis=1)
 
 
-def own_kernel(nx, ny, nz, info, own, cen_hbm, base, cx, cy, fext, qext, cen, sem):
-    centers = pltpu.make_async_copy(cen_hbm, cen, sem)
-    centers.start()
-    rows = Rows(nx, ny, nz, base, cx, cy, fext, qext)
+def own_kernel(nx, ny, nz, info, centers, own, kept_in, base, fext, qext, kept):
+    kept[...] = kept_in[...]
+    rows = Rows(nx, ny, nz, info, centers, base, fext, qext)
     for layer in range(nx):
-        rows.describe([own[k, layer] for k in range(3)], layer + 2, pl.ds(0, ny), True)
-    centers.wait()
-    rows.coefficients(info, cen)
+        rows.describe([own[k, layer] for k in range(3)], layer + 2, pl.ds(0, ny), 0, True)
     for i in range(2, nx + 2):
 
         @pl.loop(0, ny, unroll=True)
@@ -228,16 +213,16 @@
             rows.both(i, j)
 
 
-def inner_kernel(nx, ny, nz, info, across, pair, cx, cy, base_in, fext_in, qext_in, base, fext, qext, lh, gram, rh):
+def inner_kernel(nx, ny, nz, info, centers, across, pair, base_in, fext_in, qext_in, base, fext, qext, lh, gram, rh):
     del base_in, fext_in, qext_in
-    rows = Rows(nx, ny, nz, base, cx, cy, fext, qext)
+    rows = Rows(nx, ny, nz, info, centers, base, fext, qext)
     core = info[4]
     other, beyond = pair[...], across[...]
     before = jnp.where(core == 0, beyond, other)
     after = jnp.where(core == 0, other, beyond)
     for layer in range(nx):
-        rows.describe([before[k, layer] for k in range(3)], layer, pl.ds(0, ny), layer == nx - 1)
-        rows.describe([after[k, layer] for k in range(3)], layer + 2 + nx, pl.ds(0, ny), layer == 0)
+        rows.describe([before[k, layer] for k in range(3)], layer, pl.ds(0, ny), 0, layer == nx - 1)
+        rows.describe([after[k, layer] for k in range(3)], layer + 2 + nx, pl.ds(0, ny), 0, layer == 0)
     for i in (0, 1, nx + 2, nx + 3):
 
         @pl.loop(0, ny, unroll=True)
@@ -264,16 +249,16 @@
 
 
 def outer_kernel(
-    nx, ny, nz, info, odd, even, cx, cy, base_in, fext_in, qext_in, gram, base, fext, qext, lh, pay, rh
+    nx, ny, nz, info, centers, odd, even, base_in, fext_in, qext_in, gram, base, fext, qext, lh, pay, rh
 ):
     del base_in, fext_in, qext_in
-    rows = Rows(nx, ny, nz, base, cx, cy, fext, qext)
+    rows = Rows(nx, ny, nz, info, centers, base, fext, qext)
     parity = info[5]
     above = jnp.where(parity == 0, even[...], odd[...])
     below = jnp.where(parity == 0, odd[...], even[...])
     for layer in range(nx + 2):
-        rows.describe([above[k, layer] for k in range(3)], layer + 1, pl.ds(ny, 2), True)
-        rows.describe([below[k, layer] for k in range(3)], layer + 1, pl.ds(ny + 2, 2), True)
+        rows.describe([above[k, layer] for k in range(3)], layer + 1, pl.ds(ny, 2), ny, True)
+        rows.describe([below[k, layer] for k in range(3)], layer + 1, pl.ds(ny + 2, 2), -2, True)
     for i in range(1, nx + 3):
         reach = 2 if 2 <= i < nx + 2 else 1
         for j in list(range(-reach, 0)) + list(range(ny, ny + reach)):
@@ -389,6 +374,7 @@
         [at_x * nx, at_y * ny, jnp.int32(count_x), jnp.int32(count_y), core, parity]
     ).astype(jnp.int32)
     half = nx * ny * nz // 2
+    centers = body_centers.T
     ex, ey = nx + 4, ny + 4
     vmem = pl.BlockSpec(memory_space=pltpu.VMEM)
     smem = pl.BlockSpec(memory_space=pltpu.SMEM)
@@ -396,11 +382,11 @@
     def shape(*dims):
         return jax.ShapeDtypeStruct(dims, F32)
 
-    def call(kernel, outs, ins, scratch, flops, aliases, name, last=vmem):
+    def call(kernel, outs, ins, scratch, flops, aliases, name):
         return pl.pallas_call(
             functools.partial(kernel, nx, ny, nz),
             out_shape=outs,
-            in_specs=[smem] + [vmem] * (len(ins) - 2) + [last],
+            in_specs=[smem, smem] + [vmem] * (len(ins) - 2),
             out_specs=tuple(vmem for _ in outs),
             scratch_shapes=scratch,
             input_output_aliases=aliases,
@@ -409,22 +395,21 @@
             name=name,
         )(*ins)
 
-    base, field = shape(13, ex, ey, nz), shape(ex, ey, COLS, nz)
-    base, cx, cy, fext, qext = call(
-        own_kernel, (base, shape(2, ex, COLS, nz), shape(2, ey, COLS, nz), field, field),
-        (info, own, body_centers.T), [pltpu.VMEM((3, BODIES), F32), pltpu.SemaphoreType.DMA], 1 << 28, {}, "own_rows",
-        pl.BlockSpec(memory_space=pltpu.HBM),
+    base, field = shape(MASK + 1, ex, ey, nz), shape(ex, ey, COLS, nz)
+    base, fext, qext, kept = call(
+        own_kernel, (base, field, field, shape(3, BODIES)),
+        (info, centers, own, centers), [], 1 << 28, {}, "own_rows",
     )
     rh = [pltpu.VMEM((2 * COLS + FOLD, half), F32)]
     base, fext, qext, inner, gram = call(
         inner_kernel,
         (shape(*base.shape), shape(*fext.shape), shape(*qext.shape), shape(2 * COLS, half), shape(2 * COLS, 2 * COLS + FOLD)),
-        (info, across, pair, cx, cy, base, fext, qext), rh, 1 << 29, {5: 0, 6: 1, 7: 2}, "inner_rows",
+        (info, kept, across, pair, base, fext, qext), rh, 1 << 29, {4: 0, 5: 1, 6: 2}, "inner_rows",
     )
     _, _, _, outer, pay = call(
         outer_kernel,
         (shape(*base.shape), shape(*fext.shape), shape(*qext.shape), shape(2 * COLS, half), shape(COLS + THIRD, 128)),
-        (info, odd, even, cx, cy, base, fext, qext, gram), rh, 1 << 29, {5: 0, 6: 1, 7: 2}, "outer_rows",
+        (info, kept, odd, even, base, fext, qext, gram), rh, 1 << 29, {4: 0, 5: 1, 6: 2}, "outer_rows",
     )
     pay = reduced(pay)
     scale = 8.0 * BODIES / (count_x * count_y * nz)

time: 82.8 us -> 82.9 us (level)
  blocking collectives: 47.8 us -> 48.8 us
    pallas_call x3, Pallas kernels: 7.53 us -> 6.25 us  [call(): pl.pallas_call(functools.partial(kernel, nx, ny, nz), out_shape=outs, in_...]
  transfers between devices with their start and end apart: 4 -> 4, of which waited for: 0 -> 0; matrix products, arithmetic and copies ran while one was open for 0% -> 0% of each run, Pallas kernels for 6% -> 5%
where the time goes in v6:
time: 82.9 us; the launch traced here: 82.5 us
  blocking collectives  48.8 us (59%)
  starting transfers between devices  19.2 us (23%)
  Pallas kernels  12.1 us (15%)
  other arithmetic  0.83 us (1%)
    all_to_all x1, blocking collectives, reduced(): lax.all_to_all(jnp.broadcast_to(piece[None], (far,) + piece.shape), FAR,...  19.2 us
    ppermute x3, starting transfers between devices, swap(): return lax.ppermute(array, axes, pairs + [(j, i) for i, j in pairs])  17.3 us
    all_to_all x1, blocking collectives, reduced(): lax.all_to_all(part, NEAR, 0, 0, tiled=True)  17.2 us
    all_to_all x1, blocking collectives, reduced(): lax.all_to_all(jnp.broadcast_to(piece[None], (near,) + piece.shape), NEAR...  12.4 us
    pallas_call x3, Pallas kernels, call(): pl.pallas_call(functools.partial(kernel, nx, ny, nz), out_shape=outs, in_...  6.25 us
    pallas_call x1, Pallas kernels, shards(): pl.pallas_call(functools.partial(solve_kernel, nx, ny, nz, scale), out_sh...  5.85 us
    ppermute x1, starting transfers between devices, shards(): pair = lax.ppermute(own, 'c', [(0, 1), (1, 0)])  1.92 us
  transfers between devices with their start and end apart: 4, of which 0 were waited for; matrix products, arithmetic and copies ran while one was open for 0% of the time, Pallas kernels for 5%

profile of v6, /device:TPU:1, one launch (start us, length us, event | category | flops | bytes accessed | tf_op | source)
XLA Modules:
  0.0 82.5 jit_solution(16484779089901013091)
XLA Ops:
  0.6 0.7 pad_add_fusion.own
  1.4 10.2 %collective-permute-start.1 = (s32[3,2,8,128]{3,2,1,0:T(8,128)S(1)}, s32[3,2,8,128]{3,2,1,0:T(8,128)S(1)}, u32[]{:S(2)}, u32[]{:S(2)}) collective-permute-start(s32[3,2,8,128]{3,2,1,0:T(8,128)S(1)} %pad_add_fusion.own), channel_id=1, source_target_pairs={{16,32},{48,64},{80,96},{112,128},{144,160},{176,192},{208,224},{2... | collective-permute-start | bytes 73736 | tf_op jit(solution)/shard_map/ppermute | solution.py:345
  11.6 1.9 %collective-permute-start = (s32[3,2,8,128]{3,2,1,0:T(8,128)S(1)}, s32[3,2,8,128]{3,2,1,0:T(8,128)S(1)}, u32[]{:S(2)}, u32[]{:S(2)}) collective-permute-start(s32[3,2,8,128]{3,2,1,0:T(8,128)S(1)} %pad_add_fusion.own), channel_id=1, source_target_pairs={{0,16},{16,0},{1,17},{17,1},{2,18},{18,2},{3,19},{19,3},{4,20},{20... | collective-permute-start | bytes 73736 | tf_op jit(solution)/shard_map/ppermute | solution.py:365
  13.5 0.1 stack.31.info
  13.6 0.0 copy-start
  13.6 0.7 copy-done
  14.3 1.1 %own_rows.1 = (f32[22,6,12,128]{3,2,1,0:T(8,128)S(1)}, f32[6,12,96,128]{3,2,1,0:T(8,128)S(1)}, f32[6,12,96,128]{3,2,1,0:T(8,128)S(1)}, f32[3,16]{1,0:T(4,128)S(1)}) custom-call(s32[6]{0:T(128)S(1)} %stack.31.info, f32[3,16]{1,0:T(4,128)S(1)} %bitcast.16, s32[3,2,8,128]{3,2,1,0:T(8,128)S(1)} %pad_add_fusion.own, f32[3,16]{1,0:T(4,128)S(1)} %bitcast.17), custom_call_target="tpu_custom_call" | custom-call | flops 268435456 | bytes 8388608 | tf_op jit(solution)/shard_map/own_rows/pallas_call | solution.py:386
  15.4 0.0 collective-permute-done.1.across
  15.4 0.0 collective-permute-done.pair
  15.4 0.7 collective-permute-start.2
  16.1 6.4 %collective-permute-start.3 = (s32[3,4,2,128]{3,2,1,0:T(2,128)S(1)}, s32[3,4,2,128]{3,2,1,0:T(2,128)S(1)}, u32[]{:S(2)}, u32[]{:S(2)}) collective-permute-start(s32[3,4,2,128]{3,2,1,0:T(2,128)S(1)} %get-tuple-element.28), channel_id=1, source_target_pairs={{0,1},{2,3},{4,5},{6,7},{8,9},{10,11},{12,13},{14,15},{1,0},{3,2},... | collective-permute-start | bytes 36872 | tf_op jit(solution)/shard_map/ppermute | solution.py:345
  22.5 2.7 %inner_rows.1 = (f32[22,6,12,128]{3,2,1,0:T(8,128)S(1)}, f32[6,12,96,128]{3,2,1,0:T(8,128)S(1)}, f32[6,12,96,128]{3,2,1,0:T(8,128)S(1)}, f32[192,1024]{1,0:T(8,128)S(1)}, f32[192,216]{1,0:T(8,128)S(1)}) custom-call(s32[6]{0:T(128)S(1)} %stack.31.info, ...), custom_call_target="tpu_custom_call", output_to_operand_aliasing={{0}: (4, {}), {1}: (5, {}), {2}: (6, {})} | custom-call | flops 536870912 | bytes 8388608 | tf_op jit(solution)/shard_map/inner_rows/pallas_call | solution.py:386
  25.3 0.0 collective-permute-done.2.odd
  25.3 0.0 collective-permute-done.3.even
  25.3 2.5 %outer_rows.1 = (f32[22,6,12,128]{3,2,1,0:T(8,128)S(1)}, f32[6,12,96,128]{3,2,1,0:T(8,128)S(1)}, f32[6,12,96,128]{3,2,1,0:T(8,128)S(1)}, f32[192,1024]{1,0:T(8,128)S(1)}, f32[128,128]{1,0:T(8,128)S(1)}) custom-call(s32[6]{0:T(128)S(1)} %stack.31.info, ...), custom_call_target="tpu_custom_call", output_to_operand_aliasing={{0}: (4, {}), {1}: (5, {}), {2}: (6, {})} | custom-call | flops 536870912 | bytes 8388608 | tf_op jit(solution)/shard_map/outer_rows/pallas_call | solution.py:386
  27.8 17.2 %all_to_all.19 = f32[32,4,128]{2,1,0:T(4,128)S(1)} all-to-all(f32[32,4,128]{2,1,0:T(4,128)S(1)} %bitcast.15), channel_id=1, replica_groups=mesh['y'=4,'zh'=4,'c'=2,'x'=4,'zl'=4] {'y','c','x'}, dimensions={0} | all-to-all | bytes 131072 | tf_op jit(solution)/shard_map/all_to_all | solution.py:351
  45.0 19.2 %all_to_all.20 = f32[16,4,128]{2,1,0:T(4,128)S(1)} all-to-all(f32[16,4,128]{2,1,0:T(4,128)S(1)} %broadcast_in_dim.4), channel_id=1, replica_groups=mesh['y'=4,'zh'=4,'c'=2,'x'=4,'zl'=4] {'zh','zl'}, dimensions={0} | all-to-all | bytes 65536 | tf_op jit(solution)/shard_map/all_to_all | solution.py:352
  64.3 12.4 %all_to_all.21 = f32[32,4,128]{2,1,0:T(4,128)S(1)} all-to-all(f32[32,4,128]{2,1,0:T(4,128)S(1)} %broadcast_in_dim.5), channel_id=1, replica_groups=mesh['y'=4,'zh'=4,'c'=2,'x'=4,'zl'=4] {'y','c','x'}, dimensions={0} | all-to-all | bytes 131072 | tf_op jit(solution)/shard_map/all_to_all | solution.py:353
  76.7 5.8 %solve.1 = (f32[1536,128]{1,0:T(8,128)}, f32[96,96]{1,0:T(8,128)}) custom-call(f32[128,128]{1,0:T(8,128)S(1)} %bitcast.14, f32[192,1024]{1,0:T(8,128)S(1)} %get-tuple-element.24.inner, f32[192,1024]{1,0:T(8,128)S(1)} %get-tuple-element.25.outer), custom_call_target="tpu_custom_call" | custom-call | tf_op jit(solution)/shard_map/solve/pallas_call | solution.py:416
  (7 shorter events, 0.1 us)
Async XLA Ops:
  1.4 14.0 %collective-permute-start.1 = (s32[3,2,8,128]{3,2,1,0:T(8,128)S(1)}, s32[3,2,8,128]{3,2,1,0:T(8,128)S(1)}, u32[]{:S(2)}, u32[]{:S(2)}) collective-permute-start(s32[3,2,8,128]{3,2,1,0:T(8,128)S(1)} %pad_add_fusion.own), channel_id=1, source_target_pairs={{16,32},{48,64},{80,96},{112,128},{144,160},{176,192},{208,224},{2... | collective-permute-start | bytes 73736 | tf_op jit(solution)/shard_map/ppermute | solution.py:345
  11.6 3.8 %collective-permute-start = (s32[3,2,8,128]{3,2,1,0:T(8,128)S(1)}, s32[3,2,8,128]{3,2,1,0:T(8,128)S(1)}, u32[]{:S(2)}, u32[]{:S(2)}) collective-permute-start(s32[3,2,8,128]{3,2,1,0:T(8,128)S(1)} %pad_add_fusion.own), channel_id=1, source_target_pairs={{0,16},{16,0},{1,17},{17,1},{2,18},{18,2},{3,19},{19,3},{4,20},{20... | collective-permute-start | bytes 73736 | tf_op jit(solution)/shard_map/ppermute | solution.py:365
  13.6 0.7 copy-start
  15.4 9.8 %collective-permute-start.2 = (s32[3,4,2,128]{3,2,1,0:T(2,128)S(1)}, s32[3,4,2,128]{3,2,1,0:T(2,128)S(1)}, u32[]{:S(2)}, u32[]{:S(2)}) collective-permute-start(s32[3,4,2,128]{3,2,1,0:T(2,128)S(1)} %bitcast.20), channel_id=1, source_target_pairs={{1,2},{3,4},{5,6},{7,8},{9,10},{11,12},{13,14},{2,1},{4,3},{6,5},{... | collective-permute-start | bytes 36872 | tf_op jit(solution)/shard_map/ppermute | solution.py:345
  16.1 9.2 %collective-permute-start.3 = (s32[3,4,2,128]{3,2,1,0:T(2,128)S(1)}, s32[3,4,2,128]{3,2,1,0:T(2,128)S(1)}, u32[]{:S(2)}, u32[]{:S(2)}) collective-permute-start(s32[3,4,2,128]{3,2,1,0:T(2,128)S(1)} %get-tuple-element.28), channel_id=1, source_target_pairs={{0,1},{2,3},{4,5},{6,7},{8,9},{10,11},{12,13},{14,15},{1,0},{3,2},... | collective-permute-start | bytes 36872 | tf_op jit(solution)/shard_map/ppermute | solution.py:345

commit v7 on v6

--- a/solution.py
+++ b/solution.py
@@ -289,7 +289,7 @@
     rows.pack(gram[...] + dot(lh[...], rh[...], ((1,), (1,))), pay)
 
 
-def inverse_spd(matrix, work):
+def solve_spd(turned, matrix, work):
     size = matrix.shape[0]
     r = lax.broadcasted_iota(jnp.int32, (size, size), 0)
     c = lax.broadcasted_iota(jnp.int32, (size, size), 1)
@@ -297,22 +297,26 @@
     scale_r = lax.rsqrt(jnp.sum(diagonal, axis=1, keepdims=True))
     scale_c = lax.rsqrt(jnp.sum(diagonal, axis=0, keepdims=True))
     scaled = matrix * scale_r * scale_c
-    square = mm(scaled, scaled)
+    turned = turned * scale_c
+    work[0:size] = scaled
+    work[size:] = turned
+    product = mm(work[...], scaled)
+    square = product[:size]
     bound = jnp.max(jnp.sum(jnp.abs(square), axis=0, keepdims=True), axis=1, keepdims=True)
     weight = lax.rsqrt(bound)
     eye = (r == c).astype(F32)
-    work[0:size] = (30.0 / 7.0) * eye - (25.0 / 7.0 * weight) * scaled
-    work[size : 2 * size] = eye - (30.0 / 7.0 * weight) * scaled + (25.0 / 7.0 * weight * weight) * square
+    work[0:size] = eye - (30.0 / 7.0 * weight) * scaled + (25.0 / 7.0 * weight * weight) * square
+    work[size:] = (30.0 / 7.0) * turned - (25.0 / 7.0 * weight) * product[size:]
 
     def longer(carry):
-        power = work[size : 2 * size]
+        power = work[0:size]
         more = mm(work[...], power)
-        work[0:size] = work[0:size] + more[:size]
-        work[size : 2 * size] = more[size:]
+        work[0:size] = more[:size]
+        work[size:] = work[size:] + more[size:]
         return carry[0] + 1, jnp.sum(power * power) > 2e-6
 
     lax.while_loop(lambda carry: (carry[0] < 28) & carry[1], longer, (jnp.int32(0), jnp.bool_(True)))
-    return work[0:size] * (weight * scale_r) * scale_c
+    return work[size:] * (weight * scale_c)
 
 
 def solve_kernel(nx, ny, nz, scale, pay, inner, outer, out, added, work):
@@ -327,16 +331,16 @@
         ],
         axis=0,
     )
-    solved = mm(inverse_spd(energy, work), jnp.concatenate([zeroth, first - shift * zeroth], axis=0))
-    later = solved[COLS:]
-    early = solved[:COLS] - shift * later
-    coeffs = jnp.concatenate([early, later], axis=0)
+    solved = solve_spd(jnp.concatenate([zeroth, first - shift * zeroth], axis=1), energy, work)
+    later = solved[:, COLS:]
+    early = solved[:, :COLS] - shift * later
+    coeffs = jnp.concatenate([early, later], axis=1)
     rows = nx * ny
     for lh, places in ((inner, range(2, ny - 2)), (outer, [0, 1, ny - 2, ny - 1])):
-        values = dot(coeffs, lh[...], ((0,), (0,)))
+        values = mm(coeffs, lh[...])
         for k, (i, j) in enumerate((i, j) for i in range(nx) for j in places):
             out[pl.ds(i * ny + j, COLS, stride=rows), :] = values[:, k * nz : (k + 1) * nz]
-    added[...] = (mm(zeroth, early) + mm(first, later)) * scale
+    added[...] = (mm(early, zeroth) + mm(later, first)).T * scale
 
 
 def swap(array, axes, start):
@@ -421,7 +425,7 @@
         ),
         in_specs=[vmem] * 3,
         out_specs=(vmem, vmem),
-        scratch_shapes=[pltpu.VMEM((4 * COLS, 2 * COLS), F32)],
+        scratch_shapes=[pltpu.VMEM((3 * COLS, 2 * COLS), F32)],
         compiler_params=pltpu.CompilerParams(vmem_limit_bytes=24 * 1024 * 1024),
         name="solve",
     )(pay, inner, outer)

time: 82.9 us -> 82.1 us (level)
  no operation moved by 1% of the time
where the time goes in v7:
time: 82.1 us; the launch traced here: 81.7 us
  blocking collectives  48.8 us (59%)
  starting transfers between devices  19.2 us (23%)
  Pallas kernels  11.3 us (14%)
  other arithmetic  0.83 us (1%)
    all_to_all x1, blocking collectives, reduced(): lax.all_to_all(jnp.broadcast_to(piece[None], (far,) + piece.shape), FAR,...  19.2 us
    ppermute x3, starting transfers between devices, swap(): return lax.ppermute(array, axes, pairs + [(j, i) for i, j in pairs])  17.3 us
    all_to_all x1, blocking collectives, reduced(): lax.all_to_all(part, NEAR, 0, 0, tiled=True)  17.2 us
    all_to_all x1, blocking collectives, reduced(): lax.all_to_all(jnp.broadcast_to(piece[None], (near,) + piece.shape), NEAR...  12.4 us
    pallas_call x3, Pallas kernels, call(): pl.pallas_call(functools.partial(kernel, nx, ny, nz), out_shape=outs, in_...  6.25 us
    pallas_call x1, Pallas kernels, shards(): pl.pallas_call(functools.partial(solve_kernel, nx, ny, nz, scale), out_sh...  5.08 us
    ppermute x1, starting transfers between devices, shards(): pair = lax.ppermute(own, 'c', [(0, 1), (1, 0)])  1.92 us
  transfers between devices with their start and end apart: 4, of which 0 were waited for; matrix products, arithmetic and copies ran while one was open for 0% of the time, Pallas kernels for 5%

profile of v7, /device:TPU:1, one launch (start us, length us, event | category | flops | bytes accessed | tf_op | source)
XLA Modules:
  0.0 81.7 jit_solution(13436143734301809590)
XLA Ops:
  0.6 0.7 pad_add_fusion.own
  1.4 10.2 %collective-permute-start.1 = (s32[3,2,8,128]{3,2,1,0:T(8,128)S(1)}, s32[3,2,8,128]{3,2,1,0:T(8,128)S(1)}, u32[]{:S(2)}, u32[]{:S(2)}) collective-permute-start(s32[3,2,8,128]{3,2,1,0:T(8,128)S(1)} %pad_add_fusion.own), channel_id=1, source_target_pairs={{16,32},{48,64},{80,96},{112,128},{144,160},{176,192},{208,224},{2... | collective-permute-start | bytes 73736 | tf_op jit(solution)/shard_map/ppermute | solution.py:349
  11.6 1.9 %collective-permute-start = (s32[3,2,8,128]{3,2,1,0:T(8,128)S(1)}, s32[3,2,8,128]{3,2,1,0:T(8,128)S(1)}, u32[]{:S(2)}, u32[]{:S(2)}) collective-permute-start(s32[3,2,8,128]{3,2,1,0:T(8,128)S(1)} %pad_add_fusion.own), channel_id=1, source_target_pairs={{0,16},{16,0},{1,17},{17,1},{2,18},{18,2},{3,19},{19,3},{4,20},{20... | collective-permute-start | bytes 73736 | tf_op jit(solution)/shard_map/ppermute | solution.py:369
  13.5 0.1 stack.31.info
  13.6 0.0 copy-start
  13.6 0.7 copy-done
  14.3 1.1 %own_rows.1 = (f32[22,6,12,128]{3,2,1,0:T(8,128)S(1)}, f32[6,12,96,128]{3,2,1,0:T(8,128)S(1)}, f32[6,12,96,128]{3,2,1,0:T(8,128)S(1)}, f32[3,16]{1,0:T(4,128)S(1)}) custom-call(s32[6]{0:T(128)S(1)} %stack.31.info, f32[3,16]{1,0:T(4,128)S(1)} %bitcast.16, s32[3,2,8,128]{3,2,1,0:T(8,128)S(1)} %pad_add_fusion.own, f32[3,16]{1,0:T(4,128)S(1)} %bitcast.17), custom_call_target="tpu_custom_call" | custom-call | flops 268435456 | bytes 8388608 | tf_op jit(solution)/shard_map/own_rows/pallas_call | solution.py:390
  15.4 0.0 collective-permute-done.1.across
  15.4 0.0 collective-permute-done.pair
  15.4 0.7 collective-permute-start.2
  16.1 6.4 %collective-permute-start.3 = (s32[3,4,2,128]{3,2,1,0:T(2,128)S(1)}, s32[3,4,2,128]{3,2,1,0:T(2,128)S(1)}, u32[]{:S(2)}, u32[]{:S(2)}) collective-permute-start(s32[3,4,2,128]{3,2,1,0:T(2,128)S(1)} %get-tuple-element.28), channel_id=1, source_target_pairs={{0,1},{2,3},{4,5},{6,7},{8,9},{10,11},{12,13},{14,15},{1,0},{3,2},... | collective-permute-start | bytes 36872 | tf_op jit(solution)/shard_map/ppermute | solution.py:349
  22.5 2.7 %inner_rows.1 = (f32[22,6,12,128]{3,2,1,0:T(8,128)S(1)}, f32[6,12,96,128]{3,2,1,0:T(8,128)S(1)}, f32[6,12,96,128]{3,2,1,0:T(8,128)S(1)}, f32[192,1024]{1,0:T(8,128)S(1)}, f32[192,216]{1,0:T(8,128)S(1)}) custom-call(s32[6]{0:T(128)S(1)} %stack.31.info, ...), custom_call_target="tpu_custom_call", output_to_operand_aliasing={{0}: (4, {}), {1}: (5, {}), {2}: (6, {})} | custom-call | flops 536870912 | bytes 8388608 | tf_op jit(solution)/shard_map/inner_rows/pallas_call | solution.py:390
  25.3 0.0 collective-permute-done.2.odd
  25.3 0.0 collective-permute-done.3.even
  25.3 2.5 %outer_rows.1 = (f32[22,6,12,128]{3,2,1,0:T(8,128)S(1)}, f32[6,12,96,128]{3,2,1,0:T(8,128)S(1)}, f32[6,12,96,128]{3,2,1,0:T(8,128)S(1)}, f32[192,1024]{1,0:T(8,128)S(1)}, f32[128,128]{1,0:T(8,128)S(1)}) custom-call(s32[6]{0:T(128)S(1)} %stack.31.info, ...), custom_call_target="tpu_custom_call", output_to_operand_aliasing={{0}: (4, {}), {1}: (5, {}), {2}: (6, {})} | custom-call | flops 536870912 | bytes 8388608 | tf_op jit(solution)/shard_map/outer_rows/pallas_call | solution.py:390
  27.8 17.2 %all_to_all.19 = f32[32,4,128]{2,1,0:T(4,128)S(1)} all-to-all(f32[32,4,128]{2,1,0:T(4,128)S(1)} %bitcast.15), channel_id=1, replica_groups=mesh['y'=4,'zh'=4,'c'=2,'x'=4,'zl'=4] {'y','c','x'}, dimensions={0} | all-to-all | bytes 131072 | tf_op jit(solution)/shard_map/all_to_all | solution.py:355
  45.0 19.2 %all_to_all.20 = f32[16,4,128]{2,1,0:T(4,128)S(1)} all-to-all(f32[16,4,128]{2,1,0:T(4,128)S(1)} %broadcast_in_dim.4), channel_id=1, replica_groups=mesh['y'=4,'zh'=4,'c'=2,'x'=4,'zl'=4] {'zh','zl'}, dimensions={0} | all-to-all | bytes 65536 | tf_op jit(solution)/shard_map/all_to_all | solution.py:356
  64.3 12.4 %all_to_all.21 = f32[32,4,128]{2,1,0:T(4,128)S(1)} all-to-all(f32[32,4,128]{2,1,0:T(4,128)S(1)} %broadcast_in_dim.5), channel_id=1, replica_groups=mesh['y'=4,'zh'=4,'c'=2,'x'=4,'zl'=4] {'y','c','x'}, dimensions={0} | all-to-all | bytes 131072 | tf_op jit(solution)/shard_map/all_to_all | solution.py:357
  76.7 5.1 %solve.1 = (f32[1536,128]{1,0:T(8,128)}, f32[96,96]{1,0:T(8,128)}) custom-call(f32[128,128]{1,0:T(8,128)S(1)} %bitcast.14, f32[192,1024]{1,0:T(8,128)S(1)} %get-tuple-element.24.inner, f32[192,1024]{1,0:T(8,128)S(1)} %get-tuple-element.25.outer), custom_call_target="tpu_custom_call" | custom-call | tf_op jit(solution)/shard_map/solve/pallas_call | solution.py:420
  (7 shorter events, 0.1 us)
Async XLA Ops:
  1.4 14.0 %collective-permute-start.1 = (s32[3,2,8,128]{3,2,1,0:T(8,128)S(1)}, s32[3,2,8,128]{3,2,1,0:T(8,128)S(1)}, u32[]{:S(2)}, u32[]{:S(2)}) collective-permute-start(s32[3,2,8,128]{3,2,1,0:T(8,128)S(1)} %pad_add_fusion.own), channel_id=1, source_target_pairs={{16,32},{48,64},{80,96},{112,128},{144,160},{176,192},{208,224},{2... | collective-permute-start | bytes 73736 | tf_op jit(solution)/shard_map/ppermute | solution.py:349
  11.6 3.8 %collective-permute-start = (s32[3,2,8,128]{3,2,1,0:T(8,128)S(1)}, s32[3,2,8,128]{3,2,1,0:T(8,128)S(1)}, u32[]{:S(2)}, u32[]{:S(2)}) collective-permute-start(s32[3,2,8,128]{3,2,1,0:T(8,128)S(1)} %pad_add_fusion.own), channel_id=1, source_target_pairs={{0,16},{16,0},{1,17},{17,1},{2,18},{18,2},{3,19},{19,3},{4,20},{20... | collective-permute-start | bytes 73736 | tf_op jit(solution)/shard_map/ppermute | solution.py:369
  13.6 0.7 copy-start
  15.4 9.8 %collective-permute-start.2 = (s32[3,4,2,128]{3,2,1,0:T(2,128)S(1)}, s32[3,4,2,128]{3,2,1,0:T(2,128)S(1)}, u32[]{:S(2)}, u32[]{:S(2)}) collective-permute-start(s32[3,4,2,128]{3,2,1,0:T(2,128)S(1)} %bitcast.20), channel_id=1, source_target_pairs={{1,2},{3,4},{5,6},{7,8},{9,10},{11,12},{13,14},{2,1},{4,3},{6,5},{... | collective-permute-start | bytes 36872 | tf_op jit(solution)/shard_map/ppermute | solution.py:349
  16.1 9.2 %collective-permute-start.3 = (s32[3,4,2,128]{3,2,1,0:T(2,128)S(1)}, s32[3,4,2,128]{3,2,1,0:T(2,128)S(1)}, u32[]{:S(2)}, u32[]{:S(2)}) collective-permute-start(s32[3,4,2,128]{3,2,1,0:T(2,128)S(1)} %get-tuple-element.28), channel_id=1, source_target_pairs={{0,1},{2,3},{4,5},{6,7},{8,9},{10,11},{12,13},{14,15},{1,0},{3,2},... | collective-permute-start | bytes 36872 | tf_op jit(solution)/shard_map/ppermute | solution.py:349

commit v8 on v7

--- a/solution.py
+++ b/solution.py
@@ -14,7 +14,7 @@
 FOLD = 4 * MODES
 GX = ("y", "zh", "c")
 GY = ("x", "zl")
-NEAR = ("y", "c", "x")
+NEAR = ("c", "x", "y")
 FAR = ("zh", "zl")
 F32 = jnp.float32
 
@@ -45,11 +45,10 @@
     return r == lax.broadcasted_iota(jnp.int32, (size, size), 1)
 
 
-def chosen(shape, offset):
-    r = lax.broadcasted_iota(jnp.int32, shape, 0) - offset
+def same_mode(shape):
+    r = lax.broadcasted_iota(jnp.int32, shape, 0)
     c = lax.broadcasted_iota(jnp.int32, shape, 1)
-    inside = (r >= 0) & (r < FOLD)
-    return ((r - c + 2 * COLS) % MODES == 0).astype(F32) * inside.astype(F32)
+    return (c - MODES * ((c * 43) >> 8) == r).astype(F32)
 
 
 def shared(left, right):
@@ -74,7 +73,7 @@
     at = COLS + 1
     r = lax.broadcasted_iota(jnp.int32, (COLS, COLS), 0)
     c = lax.broadcasted_iota(jnp.int32, (COLS, COLS), 1)
-    zeroth = mm(pay[0:COLS, at : at + MODES], chosen((MODES, COLS), 0))
+    zeroth = mm(pay[0:COLS, at : at + MODES], same_mode((MODES, COLS)))
     zeroth = jnp.where(((r * 43) >> 8) == ((c * 43) >> 8), zeroth, 0.0)
     at, half = at + MODES, t // 2 + 1
     middle, end = unshared(
@@ -116,7 +115,8 @@
         comps = [(part - 1).astype(F32) for part in (part_x, part_y, part_z)]
         inverse = 1.0 / jnp.sqrt(comps[0] * comps[0] + comps[1] * comps[1] + comps[2] * comps[2])
         fl = fluid.astype(F32)
-        n_x, n_y, n_z = (comp * inverse * fl for comp in comps)
+        active = jnp.where(tags < BODIES, fl, 0.0)
+        n_x, n_y, n_z = (comp * inverse * active for comp in comps)
         place = [jnp.zeros(tags.shape, F32)] * 3
         for b in range(BODIES):
             here = tags == b
@@ -180,10 +180,8 @@
         lh[COLS : 2 * COLS, cells] = field
         rh[0:COLS, cells] = field
         rh[COLS : 2 * COLS, cells] = self.apply(self.qext, i, j, field, up + down)
-        fold = forcing[0:FOLD]
-        for k in range(1, COLS // FOLD):
-            fold = fold + forcing[k * FOLD : (k + 1) * FOLD]
-        rh[2 * COLS : 2 * COLS + FOLD, cells] = fold
+        for m in range(MODES):
+            rh[2 * COLS + m : 2 * COLS + m + 1, cells] = self.base[m, i, pl.ds(j, 1), :]
 
 
     @staticmethod
@@ -191,7 +189,7 @@
         first, second = grams[0:COLS, 0:COLS], grams[COLS : 2 * COLS, 0:COLS]
         third = grams[COLS : 2 * COLS, COLS : 2 * COLS]
         t = THIRD
-        zeroth = mm(grams[0:COLS, 2 * COLS : 2 * COLS + FOLD], chosen((FOLD, MODES), 0))
+        zeroth = grams[0:COLS, 2 * COLS : 2 * COLS + MODES]
         blocks = [[third[t * p : t * (p + 1), t * q : t * (q + 1)] for q in range(3)] for p in range(3)]
         ends = shared(blocks[1][1], blocks[2][2])
         half = t // 2 + 1
@@ -404,10 +402,10 @@
         own_kernel, (base, field, field, shape(3, BODIES)),
         (info, centers, own, centers), [], 1 << 28, {}, "own_rows",
     )
-    rh = [pltpu.VMEM((2 * COLS + FOLD, half), F32)]
+    rh = [pltpu.VMEM((2 * COLS + MODES, half), F32)]
     base, fext, qext, inner, gram = call(
         inner_kernel,
-        (shape(*base.shape), shape(*fext.shape), shape(*qext.shape), shape(2 * COLS, half), shape(2 * COLS, 2 * COLS + FOLD)),
+        (shape(*base.shape), shape(*fext.shape), shape(*qext.shape), shape(2 * COLS, half), shape(2 * COLS, 2 * COLS + MODES)),
         (info, kept, across, pair, base, fext, qext), rh, 1 << 29, {4: 0, 5: 1, 6: 2}, "inner_rows",
     )
     _, _, _, outer, pay = call(

time: 82.1 us -> 81.8 us (level)
  no operation moved by 1% of the time
where the time goes in v8:
time: 81.8 us; the launch traced here: 81.3 us
  blocking collectives  48.5 us (59%)
  starting transfers between devices  19.2 us (23%)
  Pallas kernels  11.2 us (14%)
  other arithmetic  0.83 us (1%)
    all_to_all x1, blocking collectives, reduced(): lax.all_to_all(jnp.broadcast_to(piece[None], (far,) + piece.shape), FAR,...  19.2 us
    ppermute x3, starting transfers between devices, swap(): return lax.ppermute(array, axes, pairs + [(j, i) for i, j in pairs])  17.3 us
    all_to_all x1, blocking collectives, reduced(): lax.all_to_all(part, NEAR, 0, 0, tiled=True)  17.1 us
    all_to_all x1, blocking collectives, reduced(): lax.all_to_all(jnp.broadcast_to(piece[None], (near,) + piece.shape), NEAR...  12.2 us
    pallas_call x3, Pallas kernels, call(): pl.pallas_call(functools.partial(kernel, nx, ny, nz), out_shape=outs, in_...  6.14 us
    pallas_call x1, Pallas kernels, shards(): pl.pallas_call(functools.partial(solve_kernel, nx, ny, nz, scale), out_sh...  5.07 us
    ppermute x1, starting transfers between devices, shards(): pair = lax.ppermute(own, 'c', [(0, 1), (1, 0)])  1.92 us
  transfers between devices with their start and end apart: 4, of which 0 were waited for; matrix products, arithmetic and copies ran while one was open for 0% of the time, Pallas kernels for 5%

profile of v8, /device:TPU:1, one launch (start us, length us, event | category | flops | bytes accessed | tf_op | source)
XLA Modules:
  0.0 81.3 jit_solution(9161029847292381249)
XLA Ops:
  0.6 0.7 pad_add_fusion.own
  1.4 10.2 %collective-permute-start.1 = (s32[3,2,8,128]{3,2,1,0:T(8,128)S(1)}, s32[3,2,8,128]{3,2,1,0:T(8,128)S(1)}, u32[]{:S(2)}, u32[]{:S(2)}) collective-permute-start(s32[3,2,8,128]{3,2,1,0:T(8,128)S(1)} %pad_add_fusion.own), channel_id=1, source_target_pairs={{16,32},{48,64},{80,96},{112,128},{144,160},{176,192},{208,224},{2... | collective-permute-start | bytes 73736 | tf_op jit(solution)/shard_map/ppermute | solution.py:347
  11.6 1.9 %collective-permute-start = (s32[3,2,8,128]{3,2,1,0:T(8,128)S(1)}, s32[3,2,8,128]{3,2,1,0:T(8,128)S(1)}, u32[]{:S(2)}, u32[]{:S(2)}) collective-permute-start(s32[3,2,8,128]{3,2,1,0:T(8,128)S(1)} %pad_add_fusion.own), channel_id=1, source_target_pairs={{0,16},{16,0},{1,17},{17,1},{2,18},{18,2},{3,19},{19,3},{4,20},{20... | collective-permute-start | bytes 73736 | tf_op jit(solution)/shard_map/ppermute | solution.py:367
  13.5 0.1 stack.31.info
  13.6 0.0 copy-start
  13.6 0.7 copy-done
  14.3 1.1 %own_rows.1 = (f32[22,6,12,128]{3,2,1,0:T(8,128)S(1)}, f32[6,12,96,128]{3,2,1,0:T(8,128)S(1)}, f32[6,12,96,128]{3,2,1,0:T(8,128)S(1)}, f32[3,16]{1,0:T(4,128)S(1)}) custom-call(s32[6]{0:T(128)S(1)} %stack.31.info, f32[3,16]{1,0:T(4,128)S(1)} %bitcast.16, s32[3,2,8,128]{3,2,1,0:T(8,128)S(1)} %pad_add_fusion.own, f32[3,16]{1,0:T(4,128)S(1)} %bitcast.17), custom_call_target="tpu_custom_call" | custom-call | flops 268435456 | bytes 8388608 | tf_op jit(solution)/shard_map/own_rows/pallas_call | solution.py:388
  15.4 0.0 collective-permute-done.1.across
  15.4 0.0 collective-permute-done.pair
  15.4 0.7 collective-permute-start.2
  16.1 6.4 %collective-permute-start.3 = (s32[3,4,2,128]{3,2,1,0:T(2,128)S(1)}, s32[3,4,2,128]{3,2,1,0:T(2,128)S(1)}, u32[]{:S(2)}, u32[]{:S(2)}) collective-permute-start(s32[3,4,2,128]{3,2,1,0:T(2,128)S(1)} %get-tuple-element.28), channel_id=1, source_target_pairs={{0,1},{2,3},{4,5},{6,7},{8,9},{10,11},{12,13},{14,15},{1,0},{3,2},... | collective-permute-start | bytes 36872 | tf_op jit(solution)/shard_map/ppermute | solution.py:347
  22.6 2.7 %inner_rows.1 = (f32[22,6,12,128]{3,2,1,0:T(8,128)S(1)}, f32[6,12,96,128]{3,2,1,0:T(8,128)S(1)}, f32[6,12,96,128]{3,2,1,0:T(8,128)S(1)}, f32[192,1024]{1,0:T(8,128)S(1)}, f32[192,198]{1,0:T(8,128)S(1)}) custom-call(s32[6]{0:T(128)S(1)} %stack.31.info, ...), custom_call_target="tpu_custom_call", output_to_operand_aliasing={{0}: (4, {}), {1}: (5, {}), {2}: (6, {})} | custom-call | flops 536870912 | bytes 8388608 | tf_op jit(solution)/shard_map/inner_rows/pallas_call | solution.py:388
  25.3 0.0 collective-permute-done.2.odd
  25.3 0.0 collective-permute-done.3.even
  25.3 2.4 %outer_rows.1 = (f32[22,6,12,128]{3,2,1,0:T(8,128)S(1)}, f32[6,12,96,128]{3,2,1,0:T(8,128)S(1)}, f32[6,12,96,128]{3,2,1,0:T(8,128)S(1)}, f32[192,1024]{1,0:T(8,128)S(1)}, f32[128,128]{1,0:T(8,128)S(1)}) custom-call(s32[6]{0:T(128)S(1)} %stack.31.info, ...), custom_call_target="tpu_custom_call", output_to_operand_aliasing={{0}: (4, {}), {1}: (5, {}), {2}: (6, {})} | custom-call | flops 536870912 | bytes 8388608 | tf_op jit(solution)/shard_map/outer_rows/pallas_call | solution.py:388
  27.7 17.1 %all_to_all.19 = f32[32,4,128]{2,1,0:T(4,128)S(1)} all-to-all(f32[32,4,128]{2,1,0:T(4,128)S(1)} %bitcast.15), channel_id=1, replica_groups=mesh['y'=4,'zh'=4,'c'=2,'x'=4,'zl'=4] {'c','x','y'}, dimensions={0} | all-to-all | bytes 131072 | tf_op jit(solution)/shard_map/all_to_all | solution.py:353
  44.8 19.2 %all_to_all.20 = f32[16,4,128]{2,1,0:T(4,128)S(1)} all-to-all(f32[16,4,128]{2,1,0:T(4,128)S(1)} %broadcast_in_dim.4), channel_id=1, replica_groups=mesh['y'=4,'zh'=4,'c'=2,'x'=4,'zl'=4] {'zh','zl'}, dimensions={0} | all-to-all | bytes 65536 | tf_op jit(solution)/shard_map/all_to_all | solution.py:354
  64.1 12.2 %all_to_all.21 = f32[32,4,128]{2,1,0:T(4,128)S(1)} all-to-all(f32[32,4,128]{2,1,0:T(4,128)S(1)} %broadcast_in_dim.5), channel_id=1, replica_groups=mesh['y'=4,'zh'=4,'c'=2,'x'=4,'zl'=4] {'c','x','y'}, dimensions={0} | all-to-all | bytes 131072 | tf_op jit(solution)/shard_map/all_to_all | solution.py:355
  76.3 5.1 %solve.1 = (f32[1536,128]{1,0:T(8,128)}, f32[96,96]{1,0:T(8,128)}) custom-call(f32[128,128]{1,0:T(8,128)S(1)} %bitcast.14, f32[192,1024]{1,0:T(8,128)S(1)} %get-tuple-element.24.inner, f32[192,1024]{1,0:T(8,128)S(1)} %get-tuple-element.25.outer), custom_call_target="tpu_custom_call" | custom-call | tf_op jit(solution)/shard_map/solve/pallas_call | solution.py:418
  (7 shorter events, 0.1 us)
Async XLA Ops:
  1.4 14.0 %collective-permute-start.1 = (s32[3,2,8,128]{3,2,1,0:T(8,128)S(1)}, s32[3,2,8,128]{3,2,1,0:T(8,128)S(1)}, u32[]{:S(2)}, u32[]{:S(2)}) collective-permute-start(s32[3,2,8,128]{3,2,1,0:T(8,128)S(1)} %pad_add_fusion.own), channel_id=1, source_target_pairs={{16,32},{48,64},{80,96},{112,128},{144,160},{176,192},{208,224},{2... | collective-permute-start | bytes 73736 | tf_op jit(solution)/shard_map/ppermute | solution.py:347
  11.6 3.8 %collective-permute-start = (s32[3,2,8,128]{3,2,1,0:T(8,128)S(1)}, s32[3,2,8,128]{3,2,1,0:T(8,128)S(1)}, u32[]{:S(2)}, u32[]{:S(2)}) collective-permute-start(s32[3,2,8,128]{3,2,1,0:T(8,128)S(1)} %pad_add_fusion.own), channel_id=1, source_target_pairs={{0,16},{16,0},{1,17},{17,1},{2,18},{18,2},{3,19},{19,3},{4,20},{20... | collective-permute-start | bytes 73736 | tf_op jit(solution)/shard_map/ppermute | solution.py:367
  13.6 0.7 copy-start
  15.4 9.8 %collective-permute-start.2 = (s32[3,4,2,128]{3,2,1,0:T(2,128)S(1)}, s32[3,4,2,128]{3,2,1,0:T(2,128)S(1)}, u32[]{:S(2)}, u32[]{:S(2)}) collective-permute-start(s32[3,4,2,128]{3,2,1,0:T(2,128)S(1)} %bitcast.20), channel_id=1, source_target_pairs={{1,2},{3,4},{5,6},{7,8},{9,10},{11,12},{13,14},{2,1},{4,3},{6,5},{... | collective-permute-start | bytes 36872 | tf_op jit(solution)/shard_map/ppermute | solution.py:347
  16.1 9.2 %collective-permute-start.3 = (s32[3,4,2,128]{3,2,1,0:T(2,128)S(1)}, s32[3,4,2,128]{3,2,1,0:T(2,128)S(1)}, u32[]{:S(2)}, u32[]{:S(2)}) collective-permute-start(s32[3,4,2,128]{3,2,1,0:T(2,128)S(1)} %get-tuple-element.28), channel_id=1, source_target_pairs={{0,1},{2,3},{4,5},{6,7},{8,9},{10,11},{12,13},{14,15},{1,0},{3,2},... | collective-permute-start | bytes 36872 | tf_op jit(solution)/shard_map/ppermute | solution.py:347

commit v9 on v8

--- a/solution.py
+++ b/solution.py
@@ -185,9 +185,9 @@
 
 
     @staticmethod
-    def pack(grams, pay):
+    def pack(grams, more, pay):
         first, second = grams[0:COLS, 0:COLS], grams[COLS : 2 * COLS, 0:COLS]
-        third = grams[COLS : 2 * COLS, COLS : 2 * COLS]
+        third = grams[COLS : 2 * COLS, COLS : 2 * COLS] + more
         t = THIRD
         zeroth = grams[0:COLS, 2 * COLS : 2 * COLS + MODES]
         blocks = [[third[t * p : t * (p + 1), t * q : t * (q + 1)] for q in range(3)] for p in range(3)]
@@ -211,7 +211,7 @@
             rows.both(i, j)
 
 
-def inner_kernel(nx, ny, nz, info, centers, across, pair, base_in, fext_in, qext_in, base, fext, qext, lh, gram, rh):
+def inner_kernel(nx, ny, nz, info, centers, across, pair, base_in, fext_in, qext_in, base, fext, qext, lh, gram, rh, lh2, rh2):
     del base_in, fext_in, qext_in
     rows = Rows(nx, ny, nz, info, centers, base, fext, qext)
     core = info[4]
@@ -243,7 +243,17 @@
             cells = pl.ds(pl.multiple_of(((i - 2) * (ny - 4) + k) * nz, nz), nz)
             rows.collect(i, k + 2, cells, lh, rh)
 
+    for k, (i, j) in enumerate((i, j) for i in range(nx) for j in (1, ny - 2)):
+        cells = slice(k * nz, (k + 1) * nz)
+        lh2[0:COLS, cells] = fext[i + 2, j]
+        lh2[COLS:, cells] = qext[i + 2, j]
+        rh2[0:COLS, cells] = qext[i + 2, j]
+        for m in range(MODES):
+            rh2[COLS + m : COLS + m + 1, cells] = base[m, i + 2, j : j + 1, :]
+    more = dot(lh2[...], rh2[...], ((1,), (1,)))
     gram[...] = dot(lh[...], rh[...], ((1,), (1,)))
+    gram[:, 0:COLS] = gram[:, 0:COLS] + more[:, 0:COLS]
+    gram[:, 2 * COLS :] = gram[:, 2 * COLS :] + more[:, COLS:]
 
 
 def outer_kernel(
@@ -277,14 +287,11 @@
             def _(k, i=i):
                 rows.operated(i, k * (ny + 1) - 1)
 
-    for i in range(2, nx + 2):
-
-        @pl.loop(0, 4, unroll=True)
-        def _(k, i=i):
-            cells = pl.ds(pl.multiple_of(((i - 2) * 4 + k) * nz, nz), nz)
-            rows.collect(i, jnp.where(k < 2, k, k + ny - 4), cells, lh, rh)
-
-    rows.pack(gram[...] + dot(lh[...], rh[...], ((1,), (1,))), pay)
+    for k, (i, j) in enumerate((i, j) for pair in ((0, ny - 1), (1, ny - 2)) for i in range(nx) for j in pair):
+        rows.collect(i + 2, j, pl.ds(k * nz, nz), lh, rh)
+    half = nx * 2 * nz
+    grams = gram[...] + dot(lh[:, 0:half], rh[:, 0:half], ((1,), (1,)))
+    rows.pack(grams, dot(lh[COLS:, half:], rh[COLS : 2 * COLS, half:], ((1,), (1,))), pay)
 
 
 def solve_spd(turned, matrix, work):
@@ -334,9 +341,11 @@
     early = solved[:, :COLS] - shift * later
     coeffs = jnp.concatenate([early, later], axis=1)
     rows = nx * ny
-    for lh, places in ((inner, range(2, ny - 2)), (outer, [0, 1, ny - 2, ny - 1])):
+    middle = [(i, j) for i in range(nx) for j in range(2, ny - 2)]
+    ends = [(i, j) for pair in ((0, ny - 1), (1, ny - 2)) for i in range(nx) for j in pair]
+    for lh, places in ((inner, middle), (outer, ends)):
         values = mm(coeffs, lh[...])
-        for k, (i, j) in enumerate((i, j) for i in range(nx) for j in places):
+        for k, (i, j) in enumerate(places):
             out[pl.ds(i * ny + j, COLS, stride=rows), :] = values[:, k * nz : (k + 1) * nz]
     added[...] = (mm(early, zeroth) + mm(later, first)).T * scale
 
@@ -406,7 +415,7 @@
     base, fext, qext, inner, gram = call(
         inner_kernel,
         (shape(*base.shape), shape(*fext.shape), shape(*qext.shape), shape(2 * COLS, half), shape(2 * COLS, 2 * COLS + MODES)),
-        (info, kept, across, pair, base, fext, qext), rh, 1 << 29, {4: 0, 5: 1, 6: 2}, "inner_rows",
+        (info, kept, across, pair, base, fext, qext), rh + [pltpu.VMEM((2 * COLS, half // 2), F32), pltpu.VMEM((COLS + MODES, half // 2), F32)], 1 << 29, {4: 0, 5: 1, 6: 2}, "inner_rows",
     )
     _, _, _, outer, pay = call(
         outer_kernel,

time: 81.8 us -> 81.5 us (level)
  no operation moved by 1% of the time
where the time goes in v9:
time: 81.5 us; the launch traced here: 81.1 us
  blocking collectives  48.4 us (59%)
  starting transfers between devices  19.2 us (24%)
  Pallas kernels  11.2 us (14%)
  other arithmetic  0.83 us (1%)
    all_to_all x1, blocking collectives, reduced(): lax.all_to_all(jnp.broadcast_to(piece[None], (far,) + piece.shape), FAR,...  19.2 us
    ppermute x3, starting transfers between devices, swap(): return lax.ppermute(array, axes, pairs + [(j, i) for i, j in pairs])  17.3 us
    all_to_all x1, blocking collectives, reduced(): lax.all_to_all(part, NEAR, 0, 0, tiled=True)  16.9 us
    all_to_all x1, blocking collectives, reduced(): lax.all_to_all(jnp.broadcast_to(piece[None], (near,) + piece.shape), NEAR...  12.2 us
    pallas_call x3, Pallas kernels, call(): pl.pallas_call(functools.partial(kernel, nx, ny, nz), out_shape=outs, in_...  6.08 us
    pallas_call x1, Pallas kernels, shards(): pl.pallas_call(functools.partial(solve_kernel, nx, ny, nz, scale), out_sh...  5.07 us
    ppermute x1, starting transfers between devices, shards(): pair = lax.ppermute(own, 'c', [(0, 1), (1, 0)])  1.92 us
  transfers between devices with their start and end apart: 4, of which 0 were waited for; matrix products, arithmetic and copies ran while one was open for 0% of the time, Pallas kernels for 5%

profile of v9, /device:TPU:1, one launch (start us, length us, event | category | flops | bytes accessed | tf_op | source)
XLA Modules:
  0.0 81.1 jit_solution(17968509453122286885)
XLA Ops:
  0.6 0.7 pad_add_fusion.own
  1.4 10.2 %collective-permute-start.1 = (s32[3,2,8,128]{3,2,1,0:T(8,128)S(1)}, s32[3,2,8,128]{3,2,1,0:T(8,128)S(1)}, u32[]{:S(2)}, u32[]{:S(2)}) collective-permute-start(s32[3,2,8,128]{3,2,1,0:T(8,128)S(1)} %pad_add_fusion.own), channel_id=1, source_target_pairs={{16,32},{48,64},{80,96},{112,128},{144,160},{176,192},{208,224},{2... | collective-permute-start | bytes 73736 | tf_op jit(solution)/shard_map/ppermute | solution.py:356
  11.6 1.9 %collective-permute-start = (s32[3,2,8,128]{3,2,1,0:T(8,128)S(1)}, s32[3,2,8,128]{3,2,1,0:T(8,128)S(1)}, u32[]{:S(2)}, u32[]{:S(2)}) collective-permute-start(s32[3,2,8,128]{3,2,1,0:T(8,128)S(1)} %pad_add_fusion.own), channel_id=1, source_target_pairs={{0,16},{16,0},{1,17},{17,1},{2,18},{18,2},{3,19},{19,3},{4,20},{20... | collective-permute-start | bytes 73736 | tf_op jit(solution)/shard_map/ppermute | solution.py:376
  13.5 0.1 stack.31.info
  13.6 0.0 copy-start
  13.6 0.7 copy-done
  14.3 1.1 %own_rows.1 = (f32[22,6,12,128]{3,2,1,0:T(8,128)S(1)}, f32[6,12,96,128]{3,2,1,0:T(8,128)S(1)}, f32[6,12,96,128]{3,2,1,0:T(8,128)S(1)}, f32[3,16]{1,0:T(4,128)S(1)}) custom-call(s32[6]{0:T(128)S(1)} %stack.31.info, f32[3,16]{1,0:T(4,128)S(1)} %bitcast.16, s32[3,2,8,128]{3,2,1,0:T(8,128)S(1)} %pad_add_fusion.own, f32[3,16]{1,0:T(4,128)S(1)} %bitcast.17), custom_call_target="tpu_custom_call" | custom-call | flops 268435456 | bytes 8388608 | tf_op jit(solution)/shard_map/own_rows/pallas_call | solution.py:397
  15.4 0.0 collective-permute-done.1.across
  15.4 0.0 collective-permute-done.pair
  15.4 0.7 collective-permute-start.2
  16.1 6.4 %collective-permute-start.3 = (s32[3,4,2,128]{3,2,1,0:T(2,128)S(1)}, s32[3,4,2,128]{3,2,1,0:T(2,128)S(1)}, u32[]{:S(2)}, u32[]{:S(2)}) collective-permute-start(s32[3,4,2,128]{3,2,1,0:T(2,128)S(1)} %get-tuple-element.28), channel_id=1, source_target_pairs={{0,1},{2,3},{4,5},{6,7},{8,9},{10,11},{12,13},{14,15},{1,0},{3,2},... | collective-permute-start | bytes 36872 | tf_op jit(solution)/shard_map/ppermute | solution.py:356
  22.6 2.9 %inner_rows.1 = (f32[22,6,12,128]{3,2,1,0:T(8,128)S(1)}, f32[6,12,96,128]{3,2,1,0:T(8,128)S(1)}, f32[6,12,96,128]{3,2,1,0:T(8,128)S(1)}, f32[192,1024]{1,0:T(8,128)S(1)}, f32[192,198]{1,0:T(8,128)S(1)}) custom-call(s32[6]{0:T(128)S(1)} %stack.31.info, ...), custom_call_target="tpu_custom_call", output_to_operand_aliasing={{0}: (4, {}), {1}: (5, {}), {2}: (6, {})} | custom-call | flops 536870912 | bytes 8388608 | tf_op jit(solution)/shard_map/inner_rows/pallas_call | solution.py:397
  25.4 0.0 collective-permute-done.2.odd
  25.4 0.0 collective-permute-done.3.even
  25.4 2.1 %outer_rows.1 = (f32[22,6,12,128]{3,2,1,0:T(8,128)S(1)}, f32[6,12,96,128]{3,2,1,0:T(8,128)S(1)}, f32[6,12,96,128]{3,2,1,0:T(8,128)S(1)}, f32[192,1024]{1,0:T(8,128)S(1)}, f32[128,128]{1,0:T(8,128)S(1)}) custom-call(s32[6]{0:T(128)S(1)} %stack.31.info, ...), custom_call_target="tpu_custom_call", output_to_operand_aliasing={{0}: (4, {}), {1}: (5, {}), {2}: (6, {})} | custom-call | flops 536870912 | bytes 8388608 | tf_op jit(solution)/shard_map/outer_rows/pallas_call | solution.py:397
  27.6 16.9 %all_to_all.19 = f32[32,4,128]{2,1,0:T(4,128)S(1)} all-to-all(f32[32,4,128]{2,1,0:T(4,128)S(1)} %bitcast.15), channel_id=1, replica_groups=mesh['y'=4,'zh'=4,'c'=2,'x'=4,'zl'=4] {'c','x','y'}, dimensions={0} | all-to-all | bytes 131072 | tf_op jit(solution)/shard_map/all_to_all | solution.py:362
  44.6 19.2 %all_to_all.20 = f32[16,4,128]{2,1,0:T(4,128)S(1)} all-to-all(f32[16,4,128]{2,1,0:T(4,128)S(1)} %broadcast_in_dim.4), channel_id=1, replica_groups=mesh['y'=4,'zh'=4,'c'=2,'x'=4,'zl'=4] {'zh','zl'}, dimensions={0} | all-to-all | bytes 65536 | tf_op jit(solution)/shard_map/all_to_all | solution.py:363
  63.8 12.2 %all_to_all.21 = f32[32,4,128]{2,1,0:T(4,128)S(1)} all-to-all(f32[32,4,128]{2,1,0:T(4,128)S(1)} %broadcast_in_dim.5), channel_id=1, replica_groups=mesh['y'=4,'zh'=4,'c'=2,'x'=4,'zl'=4] {'c','x','y'}, dimensions={0} | all-to-all | bytes 131072 | tf_op jit(solution)/shard_map/all_to_all | solution.py:364
  76.0 5.1 %solve.1 = (f32[1536,128]{1,0:T(8,128)}, f32[96,96]{1,0:T(8,128)}) custom-call(f32[128,128]{1,0:T(8,128)S(1)} %bitcast.14, f32[192,1024]{1,0:T(8,128)S(1)} %get-tuple-element.24.inner, f32[192,1024]{1,0:T(8,128)S(1)} %get-tuple-element.25.outer), custom_call_target="tpu_custom_call" | custom-call | tf_op jit(solution)/shard_map/solve/pallas_call | solution.py:427
  (7 shorter events, 0.1 us)
Async XLA Ops:
  1.4 14.0 %collective-permute-start.1 = (s32[3,2,8,128]{3,2,1,0:T(8,128)S(1)}, s32[3,2,8,128]{3,2,1,0:T(8,128)S(1)}, u32[]{:S(2)}, u32[]{:S(2)}) collective-permute-start(s32[3,2,8,128]{3,2,1,0:T(8,128)S(1)} %pad_add_fusion.own), channel_id=1, source_target_pairs={{16,32},{48,64},{80,96},{112,128},{144,160},{176,192},{208,224},{2... | collective-permute-start | bytes 73736 | tf_op jit(solution)/shard_map/ppermute | solution.py:356
  11.6 3.8 %collective-permute-start = (s32[3,2,8,128]{3,2,1,0:T(8,128)S(1)}, s32[3,2,8,128]{3,2,1,0:T(8,128)S(1)}, u32[]{:S(2)}, u32[]{:S(2)}) collective-permute-start(s32[3,2,8,128]{3,2,1,0:T(8,128)S(1)} %pad_add_fusion.own), channel_id=1, source_target_pairs={{0,16},{16,0},{1,17},{17,1},{2,18},{18,2},{3,19},{19,3},{4,20},{20... | collective-permute-start | bytes 73736 | tf_op jit(solution)/shard_map/ppermute | solution.py:376
  13.6 0.7 copy-start
  15.4 10.0 %collective-permute-start.2 = (s32[3,4,2,128]{3,2,1,0:T(2,128)S(1)}, s32[3,4,2,128]{3,2,1,0:T(2,128)S(1)}, u32[]{:S(2)}, u32[]{:S(2)}) collective-permute-start(s32[3,4,2,128]{3,2,1,0:T(2,128)S(1)} %bitcast.20), channel_id=1, source_target_pairs={{1,2},{3,4},{5,6},{7,8},{9,10},{11,12},{13,14},{2,1},{4,3},{6,5},{... | collective-permute-start | bytes 36872 | tf_op jit(solution)/shard_map/ppermute | solution.py:356
  16.1 9.3 %collective-permute-start.3 = (s32[3,4,2,128]{3,2,1,0:T(2,128)S(1)}, s32[3,4,2,128]{3,2,1,0:T(2,128)S(1)}, u32[]{:S(2)}, u32[]{:S(2)}) collective-permute-start(s32[3,4,2,128]{3,2,1,0:T(2,128)S(1)} %get-tuple-element.28), channel_id=1, source_target_pairs={{0,1},{2,3},{4,5},{6,7},{8,9},{10,11},{12,13},{14,15},{1,0},{3,2},... | collective-permute-start | bytes 36872 | tf_op jit(solution)/shard_map/ppermute | solution.py:356
